TPU v7x, 512 devices: a whole 4x8x8 slice. The times are simulated.
512 devices in a mesh: fsdp: 32 (over y, z_hi, core), ctx: 16 (over z_lo, x).
Axes of the slice: x: 4, y: 8, z: 8 (z_hi: 2, z_lo: 4; z = z_hi * 4 + z_lo), core: 2. Of those that a mesh axis runs over, the one named last changes fastest.
Arguments:
- byte_ids: int32 [32, 16384], P('fsdp', 'ctx'), may hold values from 0 to 255
- byte_table: bfloat16 [256, 768], replicated, may hold values from -6 to 6
- w_conv: bfloat16 [3072, 1024], P('fsdp'), may hold values from -0.109375 to 0.109375
- w_qkv: bfloat16 [1024, 1536], P('fsdp'), may hold values from -4 to 4
- w_out: bfloat16 [1024, 1024], P('fsdp'), may hold values from -0.1875 to 0.1875
- norm_gain: bfloat16 [1024], replicated, may hold values from 0.5 to 1.5
- teacher: bfloat16 [32, 4096, 1024], P('fsdp', 'ctx'), may hold values from -6 to 6
- align: int32 [32, 4096], P('fsdp', 'ctx'), may hold values from 0 to 4095, as said below
Outputs:
- hidden_out: bfloat16 [32, 4096, 1024], P('fsdp', 'ctx')
- token_loss: float32 [32, 4096], P('fsdp', 'ctx')
Inputs may be any that keep to these rules, and one draw needn't show every extreme that they name: Teacher token j of a sequence points at a latent of its own aligned block of 256 rows (align // 256 == j // 256); the first and the last token of each block point at that block's first and last latent.
All inputs are finite; a program needn't handle non-finite values.
Results may differ from a plain program's by a relative error of at most 0.039.
Values may be sent and summed in bfloat16 or wider, within the bound.
A program may use at most 64 MiB of HBM per device.

v0:
```python
import math

import jax
import jax.numpy as jnp
from jax import lax
from jax.sharding import PartitionSpec as P

KW = 4
HQ = 16
HK = 4
HD = 64


theta_base = 500000.0
norm_eps = 1e-05
masked_score = -1e30


def rotate(values, positions):
    half_dim = values.shape[-1] // 2
    frequency = theta_base ** (-jnp.arange(half_dim, dtype=jnp.float32) * 2.0 / values.shape[-1])
    angles = positions.astype(jnp.float32)[:, None] * frequency[None, :]
    angles = jnp.concatenate([angles, angles], axis=-1)[:, None, :]
    turned = jnp.concatenate([-values[..., half_dim:], values[..., :half_dim]], axis=-1)
    return values * jnp.cos(angles) + turned * jnp.sin(angles)


def project(inputs, weight):
    return jnp.dot(
        inputs,
        lax.all_gather(weight, "fsdp", axis=0, tiled=True),
        preferred_element_type=jnp.float32,
    )


def body(byte_ids, byte_table, w_conv, w_qkv, w_out, norm_gain, teacher, align):
    score_scale = 1.0 / math.sqrt(HD)
    seq_bytes = byte_ids.shape[1]
    lat_rows = seq_bytes // KW
    query_width = HQ * HD
    key_width = HK * HD
    one_hot = (
        byte_ids[0][:, None] == jnp.arange(byte_table.shape[0], dtype=jnp.int32)[None, :]
    ).astype(jnp.bfloat16)
    embedded = jnp.dot(one_hot, byte_table, preferred_element_type=jnp.float32).astype(jnp.bfloat16)
    stacked = embedded.reshape(lat_rows, KW * byte_table.shape[1])
    latent = project(stacked, w_conv).astype(jnp.bfloat16)
    latent_wide = latent.astype(jnp.float32)
    scale_rows = lax.rsqrt(jnp.mean(latent_wide * latent_wide, axis=1, keepdims=True) + norm_eps)
    normed = (latent_wide * scale_rows * norm_gain.astype(jnp.float32)[None, :]).astype(
        jnp.bfloat16
    )
    projected = project(normed, w_qkv)
    ctx_index = lax.axis_index("ctx")
    positions = ctx_index * lat_rows + jnp.arange(lat_rows, dtype=jnp.int32)
    queries = rotate(projected[:, :query_width].reshape(lat_rows, HQ, HD), positions).astype(
        jnp.bfloat16
    )
    key_rows = rotate(
        projected[:, query_width : query_width + key_width].reshape(lat_rows, HK, HD), positions
    )
    key_rows = key_rows.astype(jnp.bfloat16).reshape(lat_rows, key_width)
    value_rows = projected[:, query_width + key_width :].astype(jnp.bfloat16)
    grouped = queries.reshape(lat_rows, HK, HQ // HK, HD)
    start_state = (
        jnp.full((HK, HQ // HK, lat_rows), masked_score, jnp.float32),
        jnp.zeros((HK, HQ // HK, lat_rows), jnp.float32),
        jnp.zeros((HK, HQ // HK, lat_rows, HD), jnp.float32),
    )
    key_all = lax.all_gather(key_rows, "ctx", axis=0, tiled=True)
    value_all = lax.all_gather(value_rows, "ctx", axis=0, tiled=True)
    blocks = key_all.shape[0] // lat_rows
    key_blocks = key_all.reshape(blocks, lat_rows, HK, HD)
    value_blocks = value_all.reshape(blocks, lat_rows, HK, HD)
    block_starts = lat_rows * jnp.arange(blocks, dtype=jnp.int32)

    def one_block(partial_value, block_data):
        key_block, value_block, key_start = block_data
        row_top, row_mass, weighted = partial_value
        scores = (
            jnp.einsum("qkgd,skd->kgqs", grouped, key_block, preferred_element_type=jnp.float32)
            * score_scale
        )
        key_pos = key_start + jnp.arange(lat_rows, dtype=jnp.int32)
        allowed = key_pos[None, :] <= positions[:, None]
        scores = jnp.where(allowed[None, None], scores, masked_score)
        new_top = jnp.maximum(row_top, jnp.max(scores, axis=-1))
        weights = jnp.exp(scores - new_top[..., None])
        shrink = jnp.exp(row_top - new_top)
        row_mass = row_mass * shrink + jnp.sum(weights, axis=-1)
        weighted = weighted * shrink[..., None] + jnp.einsum(
            "kgqs,skd->kgqd",
            weights.astype(jnp.bfloat16),
            value_block,
            preferred_element_type=jnp.float32,
        )
        return ((new_top, row_mass, weighted), None)

    result, unused = lax.scan(one_block, start_state, (key_blocks, value_blocks, block_starts))
    final_top, final_mass, final_sum = result
    attended = final_sum / final_mass[..., None]
    attended = jnp.transpose(attended, (2, 0, 1, 3)).reshape(lat_rows, HQ * HD).astype(jnp.bfloat16)
    branch = project(attended, w_out)
    hidden_out = (latent_wide + branch).astype(jnp.bfloat16)
    local_rows = align[0] - ctx_index * lat_rows
    picked = jnp.take(hidden_out, local_rows, axis=0)
    difference = picked.astype(jnp.float32) - teacher[0].astype(jnp.float32)
    token_loss = jnp.mean(difference * difference, axis=1)
    return (hidden_out[None], token_loss[None])


def solution(mesh):
    in_specs = (
        P("fsdp", "ctx"),
        P(),
        P("fsdp", None),
        P("fsdp", None),
        P("fsdp", None),
        P(),
        P("fsdp", "ctx", None),
        P("fsdp", "ctx"),
    )
    out_specs = (P("fsdp", "ctx", None), P("fsdp", "ctx"))
    return jax.shard_map(body, mesh=mesh, in_specs=in_specs, out_specs=out_specs, check_vma=False)
```

profile of v0, /device:TPU:16, one launch (start us, length us, event | category | flops | bytes accessed | tf_op | source)
XLA Modules:
  0.0 600.0 jit_solution(9305437563675735422)
XLA Ops:
  12.9 123.3 %all-gather.6.cloned.1.call-done = bf16[3072,1024]{1,0:T(8,128)(2,1)} async-done(((bf16[96,1024]{1,0:T(8,128)(2,1)}), bf16[3072,1024]{1,0:T(8,128)(2,1)}) %all-gather.6.cloned.1.call-update) | async-done | bytes 6291472 | tf_op jit(solution)/shard_map/all_gather | solution.py:31
  136.1 5.1 fusion.22
  141.3 92.4 %all-gather.8.cloned.1.call-done = bf16[1024,1536]{1,0:T(8,128)(2,1)} async-done(((bf16[32,1536]{1,0:T(8,128)(2,1)}), bf16[1024,1536]{1,0:T(8,128)(2,1)}) %all-gather.8.cloned.1.call-update) | async-done | bytes 3145744 | tf_op jit(solution)/shard_map/all_gather | solution.py:31
  245.3 73.6 %all-gather.10.cloned.1.call-done = bf16[4096,256]{1,0:T(8,128)(2,1)} async-done(((bf16[256,256]{1,0:T(8,128)(2,1)}), bf16[4096,256]{1,0:T(8,128)(2,1)}) %all-gather.10.cloned.1.call-update) | async-done | bytes 2097168 | tf_op jit(solution)/shard_map/all_gather | solution.py:70
  318.9 7.1 %reshape.195 = bf16[16,256,4,64]{3,2,1,0:T(4,128)(2,1)} reshape(bf16[4096,256]{1,0:T(8,128)(2,1)} %all-gather.10.cloned.1.call-done) | data formatting | bytes 4194304 | tf_op jit(solution)/shard_map/reshape | solution.py:73
  326.0 6.8 %copy.26 = bf16[16,256,4,64]{1,3,2,0:T(8,128)(2,1)} copy(bf16[16,256,4,64]{3,2,1,0:T(4,128)(2,1)} %reshape.195) | data formatting | bytes 4194304
  332.8 72.6 %all-gather.12.cloned.1.call-done = bf16[4096,256]{1,0:T(8,128)(2,1)} async-done(((bf16[256,256]{1,0:T(8,128)(2,1)}), bf16[4096,256]{1,0:T(8,128)(2,1)}) %all-gather.12.cloned.1.call-update) | async-done | bytes 2097168 | tf_op jit(solution)/shard_map/all_gather | solution.py:71
  405.4 7.1 %reshape.196 = bf16[16,256,4,64]{3,2,1,0:T(4,128)(2,1)} reshape(bf16[4096,256]{1,0:T(8,128)(2,1)} %all-gather.12.cloned.1.call-done) | data formatting | bytes 4194304 | tf_op jit(solution)/shard_map/reshape | solution.py:74
  412.4 6.8 %copy.27 = bf16[16,256,4,64]{1,3,2,0:T(8,128)(2,1)} copy(bf16[16,256,4,64]{3,2,1,0:T(4,128)(2,1)} %reshape.196) | data formatting | bytes 4194304
  419.2 169.3 %while.15 = (s32[]{:T(128)}, f32[4,4,256]{2,1,0:T(4,128)S(1)}, f32[4,4,256]{2,1,0:T(4,128)S(1)}, f32[4,4,256,64]{2,3,1,0:T(8,128)S(1)}, s32[16]{0:T(128)S(1)}, /...) while((s32[]{:T(128)}, f32[4,4,256]{2,1,0:T(4,128)S(1)}, ...), condition=%wide.region_4.5_spmd.clone, body=%wide.region_1.4_spmd.clone.sunk | while | flops 280842752 | bytes 32773288 | solution.py:99
  420.6 3.6 fusion.53
  424.2 3.2 fusion.54
  431.2 3.6 fusion.53
  434.8 3.2 fusion.54
  441.7 3.6 fusion.53
  445.4 3.2 fusion.54
  452.3 3.6 fusion.53
  456.0 3.2 fusion.54
  462.9 3.6 fusion.53
  473.5 3.6 fusion.53
  484.1 3.6 fusion.53
  487.7 3.2 fusion.54
  494.7 3.6 fusion.53
  498.4 3.2 fusion.54
  505.3 3.6 fusion.53
  515.9 3.6 fusion.53
  526.5 3.6 fusion.53
  537.1 3.6 fusion.53
  547.6 3.6 fusion.53
  558.2 3.6 fusion.53
  568.8 3.6 fusion.53
  579.4 3.6 fusion.53
  (217 shorter events, 113.2 us)
Async XLA Ops:
  7.2 1.6 copy-start
  7.2 4.7 copy-start.7
  7.2 128.9 %all-gather.6.cloned.1.call-start = ((), (), s32[]{:S(2)}) async-start(), calls=%async_computation | async-start | bytes 6488064 | tf_op jit(solution)/shard_map/all_gather | solution.py:31
  7.9 225.8 %all-gather.8.cloned.1.call-start = ((), (), s32[]{:S(2)}) async-start(), calls=%async_computation.1 | async-start | bytes 3244032 | tf_op jit(solution)/shard_map/all_gather | solution.py:31
  8.7 310.3 %all-gather.10.cloned.1.call-start = ((), (), s32[]{:S(2)}) async-start(), calls=%async_computation.2 | async-start | bytes 2228224 | tf_op jit(solution)/shard_map/all_gather | solution.py:70
  12.1 0.6 copy-start.4
  12.1 224.7 %copy-start.5 = (f32[256,64]{0,1:T(8,128)}, f32[256,64]{0,1:T(8,128)S(1)}, u32[]{:S(2)}) copy-start(f32[256,64]{0,1:T(8,128)S(1)} %get-tuple-element.134) | copy-start | bytes 196612
  237.7 167.6 %all-gather.12.cloned.1.call-start = ((), (), s32[]{:S(2)}) async-start(), calls=%async_computation.3 | async-start | bytes 2228224 | tf_op jit(solution)/shard_map/all_gather | solution.py:71
  238.5 350.2 %all-gather.14.cloned.1.call-start = ((), (), s32[]{:S(2)}) async-start(), calls=%async_computation.4 | async-start | bytes 2162688 | tf_op jit(solution)/shard_map/all_gather | solution.py:31
  412.4 6.8 %copy-start.3 = (f32[4,4,256]{2,1,0:T(4,128)S(1)}, f32[4,4,256]{2,1,0:T(4,128)}, u32[]{:S(2)}) copy-start(f32[4,4,256]{2,1,0:T(4,128)} %custom-call.1) | copy-start | bytes 49156
  412.4 6.8 %copy-start.9 = (s32[16]{0:T(128)S(1)}, s32[16]{0:T(128)}, u32[]{:S(2)}) copy-start(s32[16]{0:T(128)} %iota_multiply_fusion) | copy-start | bytes 196
  424.2 3.5 copy-start.1
  434.8 3.4 copy-start.1
  445.4 3.5 copy-start.1
  455.9 3.4 copy-start.1
  466.5 3.5 copy-start.1
  477.1 3.5 copy-start.1
  487.7 3.5 copy-start.1
  498.4 3.5 copy-start.1
  508.9 3.4 copy-start.1
  519.5 3.4 copy-start.1
  530.1 3.4 copy-start.1
  540.7 3.4 copy-start.1
  551.2 3.4 copy-start.1
  561.8 3.4 copy-start.1
  572.4 3.4 copy-start.1
  583.0 3.4 copy-start.1
  588.7 3.7 copy-start.6
  588.7 3.7 copy-start.8
  591.1 2.3 copy-start.2
Sparse Core Ops, SparseCore 0:
  11.3 124.7 all-gather.5
  139.4 94.2 all-gather.7
  237.9 81.0 all-gather.9
  320.9 84.4 all-gather.11
  408.5 91.2 all-gather.13
where the time goes:
time: 602 us; the launch traced here: 600 us
  waiting for transfers between devices  364 us (60%)
  matrix products  104 us (17%)
  other arithmetic  69.7 us (12%)
  local copies, waits for them, and re-layouts  47.7 us (8%)
  between operations  14 us (2%)
    all_gather x3, waiting for transfers between devices, project(): lax.all_gather(weight, 'fsdp', axis=0, tiled=True)  216 us
    all_gather x1, waiting for transfers between devices, body(): key_all = lax.all_gather(key_rows, 'ctx', axis=0, tiled=True)  73.6 us
    all_gather x1, waiting for transfers between devices, body(): value_all = lax.all_gather(value_rows, 'ctx', axis=0, tiled=True)  72.6 us
    dot_general x16, matrix products, one_block(): jnp.einsum('qkgd,skd->kgqs', grouped, key_block, preferred_element_type=j...  57.8 us
    reduce_sum x16, other arithmetic, one_block(): row_mass = row_mass * shrink + jnp.sum(weights, axis=-1)  51.6 us
    dot_general x16, matrix products, one_block(): jnp.einsum('kgqs,skd->kgqd', weights.astype(jnp.bfloat16), value_block, p...  34.1 us
    unnamed x20, local copies, waits for them, and re-layouts  14.2 us
  transfers between devices with their start and end apart: 5, of which 4 were waited for; matrix products, arithmetic and copies ran while one was open for 35% of the time, Pallas kernels for 0%

commit v1 on v0

v1 whole, which is shorter than its diff:
```python
import math

import jax
import jax.numpy as jnp
import numpy as np
from jax import lax
from jax.experimental import pallas as pl
from jax.experimental.pallas import tpu as pltpu
from jax.sharding import PartitionSpec as P

KW = 4
HQ = 16
HK = 4
HD = 64
D = 1024
BLK = 256
NCTX = 16
theta_base = 500000.0
norm_eps = 1e-05
masked_score = -1e30
MESH = pl.DeviceIdType.MESH
F32 = jnp.float32
BF16 = jnp.bfloat16


def rope_tables(length):
    half = HD // 2
    frequency = theta_base ** (-np.arange(half, dtype=np.float64) * 2.0 / HD)
    angles = frequency[:, None] * np.arange(length, dtype=np.float64)[None, :]
    return np.cos(angles).astype(np.float32), np.sin(angles).astype(np.float32)


def rc(src, dst, send, recv, dev):
    return pltpu.make_async_remote_copy(
        src_ref=src, dst_ref=dst, send_sem=send, recv_sem=recv, device_id=dev, device_id_type=MESH
    )


def tn(a, b):
    return lax.dot_general(a, b, (((0,), (0,)), ((), ())), preferred_element_type=F32)


def kernel(
    ids_ref, bt_ref, wc_ref, wq_ref, wo_ref, cos_ref, sin_ref, teach_ref, align_ref,
    hid_ref, loss_ref,
    ids_all, scale_all, wc_all, tt, wg, wo, ut, k_scr, vt_scr, qt_scr, lat_scr, att_out, att_in,
    ids_s, ids_r, sc_s, sc_r, wc_s, wc_r, ty_s, ty_r, t3_s, t3_r, t4_s, t4_r, t5_s, t5_r,
    wg_s, wg_r, wgx_s, wgx_r, wo_s, wo_r, wo2_s, wo2_r, wo3_s, wo3_r, at_s, at_r,
):
    f = lax.axis_index("fsdp")
    c = lax.axis_index("ctx")
    g, core = f // 2, f % 2
    y, zh = f // 4, (f // 2) % 2
    zl, x = c // 4, c % 4
    tap = f // 8
    sib = (f // 2) * 2 + 1 - core
    zfull = zh * 4 + zl

    def same_core(i):
        return (((g + i) % 16) * 2 + core, c)

    def ctx_peer(i):
        return (f, (c + i) % NCTX)

    def mate(i):
        return (tap * 8 + (f % 8 + i) % 8, c)

    def z_dev(step):
        z2 = (zfull + step + 8) % 8
        return (y * 4 + (z2 // 4) * 2 + core, (z2 % 4) * 4 + x)

    def x_dev(step):
        return (f, zl * 4 + (x + step + 4) % 4)

    barrier = pltpu.get_barrier_semaphore()

    def sig(dev):
        pl.semaphore_signal(barrier, inc=1, device_id=dev, device_id_type=MESH)

    def loop(lo, hi, fn):
        def step(i, carry):
            fn(i)
            return carry

        lax.fori_loop(lo, hi, step, 0)

    loop(1, 16, lambda i: sig(same_core(i)))
    loop(1, 16, lambda i: sig(ctx_peer(i)))
    loop(1, 8, lambda i: sig(mate(i)))
    sig((sib, c))
    sig(z_dev(1))
    sig(z_dev(-1))
    sig(z_dev(-2))
    pl.semaphore_wait(barrier, 15 + 15 + 7 + 1 + 3)

    def wc_copy(i, slot):
        return rc(wc_ref, wc_all.at[slot], wc_s.at[i], wc_r.at[i], mate(i))

    loop(1, 8, lambda i: wc_copy(i, f % 8).start())
    wc_all[f % 8] = wc_ref[...]

    def ids_copy(i, slot):
        return rc(ids_ref, ids_all.at[slot], ids_s.at[i], ids_r.at[i], ctx_peer(i))

    loop(1, 16, lambda i: ids_copy(i, c).start())
    ids_all[c] = ids_ref[...]

    def wg_copy(i, slot):
        return rc(wq_ref, wg.at[slot, core], wg_s.at[i], wg_r.at[i], same_core(i))

    loop(1, 16, lambda i: wg_copy(i, g).start())
    wg[g, core] = wq_ref[...]

    btt = bt_ref[...].T
    bta = jnp.concatenate([btt[m * 96 : m * 96 + 48] for m in range(8)], axis=0)
    btb = jnp.concatenate([btt[m * 96 + 48 : m * 96 + 96] for m in range(8)], axis=0)

    loop(1, 8, lambda i: wc_copy(i, (f % 8 - i + 8) % 8).wait_recv())
    wc_val = wc_all[...].reshape(384, 128)
    piece = tn(wc_val, bta)[:64] + tn(wc_val, btb)[64:]
    half = pl.ds(pl.multiple_of(core * 512, 512), 512)

    def y_dev(step):
        return (((y + 2 * step) % 8) * 4 + zh * 2 + core, c)

    def y_copy(step, from_tap):
        ref = tt.at[zl, x, :, pl.ds(pl.multiple_of(from_tap * 256, 256), 256)]
        return rc(ref, ref, ty_s.at[step], ty_r.at[step], y_dev(step))

    @pl.when(tap // 2 == core)
    def _():
        tt[zl, x, :, pl.ds(pl.multiple_of(tap * 256, 256), 256)] = piece.astype(BF16)
        for step in (1, 2, 3):
            y_copy(step, tap).start()

    for step in (1, 2, 3):
        src_tap = (tap - step + 4) % 4

        @pl.when(src_tap // 2 == core)
        def _():
            y_copy(step, src_tap).wait_recv()

    own = tt.at[zl, x, :, half]

    def first_copy(n, dev, ref):
        return rc(ref, ref, t3_s.at[n], t3_r.at[n], dev)

    steps = (1, -1, 2)

    @pl.when(core == 0)
    def _():
        for n, s in enumerate(steps):
            first_copy(n, z_dev(s), own).start()
        for n, s in enumerate(steps):
            first_copy(n, z_dev(s), tt.at[(zl - s + 4) % 4, x, :, half]).wait_recv()
        for n, s in enumerate(steps):
            ref = tt.at[:, x, :, half]
            rc(ref, ref, t4_s.at[n], t4_r.at[n], x_dev(s)).start()

    @pl.when(core == 1)
    def _():
        for n, s in enumerate(steps):
            first_copy(n, x_dev(s), own).start()
        for n, s in enumerate(steps):
            first_copy(n, x_dev(s), tt.at[zl, (x - s + 4) % 4, :, half]).wait_recv()
        for n, s in enumerate(steps):
            ref = tt.at[zl, :, :, half]
            rc(ref, ref, t4_s.at[n], t4_r.at[n], z_dev(s)).start()

    loop(1, 16, lambda i: wg_copy(i, (g - i + 16) % 16).wait_recv())
    rc(wg.at[:, core], wg.at[:, core], wgx_s.at[0], wgx_r.at[0], (sib, c)).start()

    def wo_copy(i, slot):
        return rc(
            wo_ref.at[:, pl.ds(pl.multiple_of(x * 256, 256), 256)],
            wo.at[x, slot, core], wo_s.at[i], wo_r.at[i], same_core(i),
        )

    loop(1, 16, lambda i: wo_copy(i, g).start())
    wo[x, g, core] = wo_ref[:, pl.ds(pl.multiple_of(x * 256, 256), 256)]

    @pl.when(core == 0)
    def _():
        ref = tt.at[:, x, :, half]
        rc(ref, ref, t5_s.at[0], t5_r.at[0], (sib, c)).start()
        for n, s in enumerate(steps):
            ref = tt.at[:, (x - s + 4) % 4, :, half]
            rc(ref, ref, t4_s.at[n], t4_r.at[n], x_dev(s)).wait_recv()
            rc(ref, ref, t5_s.at[n + 1], t5_r.at[n + 1], (sib, c)).start()
        other = pl.ds(512, 512)
        for n, s in enumerate((0,) + steps):
            ref = tt.at[(zl - s + 4) % 4, :, :, other]
            rc(ref, ref, t5_s.at[n], t5_r.at[n], (sib, c)).wait_recv()

    @pl.when(core == 1)
    def _():
        ref = tt.at[zl, :, :, half]
        rc(ref, ref, t5_s.at[0], t5_r.at[0], (sib, c)).start()
        for n, s in enumerate(steps):
            ref = tt.at[(zl - s + 4) % 4, :, :, half]
            rc(ref, ref, t4_s.at[n], t4_r.at[n], z_dev(s)).wait_recv()
            rc(ref, ref, t5_s.at[n + 1], t5_r.at[n + 1], (sib, c)).start()
        other = pl.ds(0, 512)
        for n, s in enumerate((0,) + steps):
            ref = tt.at[:, (x - s + 4) % 4, :, other]
            rc(ref, ref, t5_s.at[n], t5_r.at[n], (sib, c)).wait_recv()

    def one_hot(b):
        rows = lax.broadcasted_iota(jnp.int32, (256, BLK), 0)
        block = ids_all[b]
        return jnp.concatenate(
            [(block[k : k + 1, :] == rows).astype(BF16) for k in range(KW)], axis=0
        )

    tall = tt[...].reshape(D, D)
    latent = jnp.dot(tall, one_hot(c), preferred_element_type=F32).astype(BF16)
    wide = latent.astype(F32)
    scale = lax.rsqrt(jnp.sum(wide * wide, axis=0, keepdims=True) * (1.0 / D) + norm_eps)
    scale_all[c] = scale

    def sc_copy(i, slot):
        ref = scale_all.at[slot]
        return rc(ref, ref, sc_s.at[i], sc_r.at[i], ctx_peer(i))

    loop(1, 16, lambda i: sc_copy(i, c).start())
    lat_scr[...] = latent.T

    ref = wg.at[:, 1 - core]
    rc(ref, ref, wgx_s.at[0], wgx_r.at[0], (sib, c)).wait_recv()
    ut[...] = tn(wg[...].reshape(D, 384), tall).astype(BF16)

    loop(1, 16, lambda i: wo_copy(i, (g - i + 16) % 16).wait_recv())

    def wo2_copy(n, s, slot):
        ref = wo.at[slot, :, core]
        return rc(ref, ref, wo2_s.at[n], wo2_r.at[n], x_dev(s))

    for n, s in enumerate(steps):
        wo2_copy(n, s, x).start()

    loop(1, 16, lambda i: ids_copy(i, (c - i + NCTX) % NCTX).wait_recv())
    loop(1, 16, lambda i: sc_copy(i, (c - i + NCTX) % NCTX).wait_recv())

    def turn(v, b, scale_row):
        cols = pl.ds(pl.multiple_of(b * BLK, BLK), BLK)
        cos, sin = cos_ref[:, cols] * scale_row, sin_ref[:, cols] * scale_row
        lo, hi = v[:32], v[32:]
        return jnp.concatenate([lo * cos - hi * sin, hi * cos + lo * sin], axis=0)

    def make_kv(b, carry):
        cols = pl.ds(pl.multiple_of(b * BLK, BLK), BLK)
        kv = jnp.dot(ut[256:384, :], one_hot(b), preferred_element_type=F32)
        k_scr[pl.ds(pl.multiple_of(b * BLK, BLK), BLK), :] = turn(kv[:64], b, scale_all[b]).T.astype(BF16)
        vt_scr[:64, cols] = (kv[64:] * scale_all[b]).astype(BF16)
        return carry

    vt_scr[64:, :] = jnp.ones_like(vt_scr[64:, :])
    lax.fori_loop(0, 13 + x, make_kv, 0)

    def make_q(zb, carry):
        b = zb * 4 + x
        q = jnp.dot(ut[:256, :], one_hot(b), preferred_element_type=F32)
        row = scale_all[b] * (math.log2(math.e) / math.sqrt(HD))
        for h in range(4):
            qt_scr[zb, :, h * BLK : (h + 1) * BLK] = turn(q[h * HD : (h + 1) * HD], b, row).astype(BF16)
        return carry

    lax.fori_loop(0, 4, make_q, 0)

    def scores(zb, i, h):
        keys = k_scr[pl.ds(pl.multiple_of(i * BLK, BLK), BLK), :]
        return jnp.dot(keys, qt_scr[zb, :, h * BLK : (h + 1) * BLK], preferred_element_type=F32)

    def soft(i, s, state):
        top, acc = state
        new_top = jnp.maximum(top, jnp.max(s, axis=0, keepdims=True))
        probs = jnp.exp2(s - new_top).astype(BF16)
        values = vt_scr[:, pl.ds(pl.multiple_of(i * BLK, BLK), BLK)]
        acc = acc * jnp.exp2(top - new_top) + jnp.dot(values, probs, preferred_element_type=F32)
        return new_top, acc

    def attend(zb):
        n = zb * 4 + x

        def one(i, carry):
            states, now = carry
            later = [scores(zb, i + 1, h) for h in range(4)]
            return [soft(i, now[h], states[h]) for h in range(4)], later

        def four(j, carry):
            for k in range(4):
                carry = one(j * 4 + k, carry)
            return carry

        carry = (
            [(jnp.full((1, BLK), masked_score, F32), jnp.zeros((80, BLK), F32)) for _ in range(4)],
            [scores(zb, 0, h) for h in range(4)],
        )
        carry = lax.fori_loop(0, zb, four, carry)
        states, now = lax.fori_loop(4 * zb, n, one, carry)
        rows = lax.broadcasted_iota(jnp.int32, (BLK, BLK), 0)
        cols = lax.broadcasted_iota(jnp.int32, (BLK, BLK), 1)
        outs = []
        for h in range(4):
            _, acc = soft(n, jnp.where(rows <= cols, now[h], masked_score), states[h])
            outs.append((acc[:HD] / acc[HD : HD + 1]).astype(BF16))
        return jnp.concatenate(outs, axis=0)

    def att_copy(i, zb, slot):
        return rc(att_out.at[i], att_in.at[slot], at_s.at[i], at_r.at[i], (f, zb * 4 + x))

    def other_block(i, carry):
        zb = (zl + i) % 4
        att_out[i] = attend(zb)
        att_copy(i, zb, zl).start()
        return carry

    lax.fori_loop(1, 4, other_block, 0)

    for n, s in enumerate(steps):
        wo2_copy(n, s, (x - s + 4) % 4).wait_recv()
    rc(wo.at[:, :, core], wo.at[:, :, core], wo3_s.at[0], wo3_r.at[0], (sib, c)).start()

    att_in[zl] = attend(zl)

    ref = wo.at[:, :, 1 - core]
    rc(ref, ref, wo3_s.at[0], wo3_r.at[0], (sib, c)).wait_recv()
    for i in (1, 2, 3):
        slot = (zl - i + 4) % 4
        att_copy(i, slot, slot).wait_recv()

    attended = att_in[...].reshape(D, BLK)
    pick = (align_ref[...] - c * BLK == lax.broadcasted_iota(jnp.int32, (BLK, BLK), 0)).astype(BF16)
    total = jnp.zeros((BLK, 1), F32)
    for j in range(4):
        cols = pl.ds(j * 256, 256)
        branch = tn(attended, wo[j].reshape(D, 256))
        hidden = (lat_scr[:, cols].astype(F32) + branch).astype(BF16)
        hid_ref[:, cols] = hidden
        diff = tn(pick, hidden) - teach_ref[:, cols].astype(F32)
        total = total + jnp.sum(diff * diff, axis=1, keepdims=True)
    loss_ref[...] = jnp.broadcast_to(total * (1.0 / D), (BLK, 128)).T[0:1, :]

    loop(1, 8, lambda i: wc_copy(i, f % 8).wait_send())
    loop(1, 16, lambda i: ids_copy(i, c).wait_send())
    loop(1, 16, lambda i: wg_copy(i, g).wait_send())
    loop(1, 16, lambda i: wo_copy(i, g).wait_send())
    loop(1, 16, lambda i: sc_copy(i, c).wait_send())

    @pl.when(tap // 2 == core)
    def _():
        for step in (1, 2, 3):
            y_copy(step, tap).wait_send()

    for n, s in enumerate(steps):
        first_copy(n, z_dev(s), own).wait_send()
        ref = tt.at[:, x, :, half]
        rc(ref, ref, t4_s.at[n], t4_r.at[n], x_dev(s)).wait_send()
        wo2_copy(n, s, x).wait_send()
    for n in range(4):
        ref = tt.at[:, x, :, half]
        rc(ref, ref, t5_s.at[n], t5_r.at[n], (sib, c)).wait_send()
    rc(wg.at[:, core], wg.at[:, core], wgx_s.at[0], wgx_r.at[0], (sib, c)).wait_send()
    rc(wo.at[:, :, core], wo.at[:, :, core], wo3_s.at[0], wo3_r.at[0], (sib, c)).wait_send()
    for i in (1, 2, 3):
        att_copy(i, zl, zl).wait_send()


def body(byte_ids, byte_table, w_conv, w_qkv, w_out, norm_gain, teacher, align):
    f = lax.axis_index("fsdp")
    c = lax.axis_index("ctx")
    zl = c // 4
    ids = byte_ids[0].reshape(BLK, KW).T
    wc = lax.dynamic_slice_in_dim(w_conv, c * 64, 64, axis=1)
    wc = jnp.concatenate([wc[:48], wc[48:]], axis=1)
    wq = jnp.concatenate(
        [
            lax.dynamic_slice_in_dim(w_qkv, zl * 256, 256, axis=1),
            lax.dynamic_slice_in_dim(w_qkv, HQ * HD + zl * HD, HD, axis=1),
            lax.dynamic_slice_in_dim(w_qkv, (HQ + HK) * HD + zl * HD, HD, axis=1),
        ],
        axis=1,
    )
    gain = lax.dynamic_slice_in_dim(norm_gain, f * 32, 32, axis=0)
    wq = (wq.astype(F32) * gain.astype(F32)[:, None]).astype(BF16)
    cos, sin = rope_tables(NCTX * BLK)
    vm = pl.BlockSpec(memory_space=pltpu.VMEM)
    dma = pltpu.SemaphoreType.DMA
    hidden, loss = pl.pallas_call(
        kernel,
        out_shape=(
            jax.ShapeDtypeStruct((BLK, D), BF16),
            jax.ShapeDtypeStruct((1, BLK), F32),
        ),
        in_specs=[vm] * 9,
        out_specs=(vm, vm),
        scratch_shapes=[
            pltpu.VMEM((NCTX, KW, BLK), jnp.int32),
            pltpu.VMEM((NCTX, 1, BLK), F32),
            pltpu.VMEM((8, 48, 128), BF16),
            pltpu.VMEM((4, 4, 64, 1024), BF16),
            pltpu.VMEM((16, 2, 32, 384), BF16),
            pltpu.VMEM((4, 16, 2, 32, 256), BF16),
            pltpu.VMEM((384, 1024), BF16),
            pltpu.VMEM((NCTX * BLK, HD), BF16),
            pltpu.VMEM((80, NCTX * BLK), BF16),
            pltpu.VMEM((4, HD, 4 * BLK), BF16),
            pltpu.VMEM((BLK, D), BF16),
            pltpu.VMEM((4, BLK, BLK), BF16),
            pltpu.VMEM((4, BLK, BLK), BF16),
        ]
        + [
            dma((n,))
            for n in (16, 16, 16, 16, 8, 8, 4, 4, 3, 3, 3, 3, 4, 4, 16, 16, 1, 1, 16, 16, 3, 3, 1, 1, 4, 4)
        ],
        compiler_params=pltpu.CompilerParams(
            collective_id=0, has_side_effects=True, vmem_limit_bytes=56 * 2**20
        ),
    )(ids, byte_table, wc, wq, w_out, jnp.asarray(cos), jnp.asarray(sin), teacher[0], align)
    return hidden[None], loss


def solution(mesh):
    in_specs = (
        P("fsdp", "ctx"),
        P(),
        P("fsdp", None),
        P("fsdp", None),
        P("fsdp", None),
        P(),
        P("fsdp", "ctx", None),
        P("fsdp", "ctx"),
    )
    out_specs = (P("fsdp", "ctx", None), P("fsdp", "ctx"))
    return jax.shard_map(body, mesh=mesh, in_specs=in_specs, out_specs=out_specs, check_vma=False)
```

time: 602 us -> 102 us (0.17)
  the two profiles are of different devices: /device:TPU:16 before, /device:TPU:63 now
where the time goes in v1:
time: 102 us
  Pallas kernels  92 us (90%)
  local copies, waits for them, and re-layouts  6.07 us (6%)
  other arithmetic  2.78 us (3%)
    pallas_call x1, Pallas kernels, body(): pl.pallas_call(kernel, out_shape=(jax.ShapeDtypeStruct((BLK, D), BF16), j...  92 us
    unnamed x7, local copies, waits for them, and re-layouts  2.95 us

profile of v1, /device:TPU:63, one launch (start us, length us, event | category | flops | bytes accessed | tf_op | source)
XLA Modules:
  0.0 101.6 jit_solution(15312518651269023933)
XLA Ops:
  0.7 0.0 copy-start
  0.7 0.8 dynamic-slice_convert_fusion
  1.4 0.5 broadcast.5
  1.9 0.0 copy-done
  1.9 0.7 reduce.3
  2.6 0.8 constant_dynamic-slice_fusion.2
  3.4 0.7 constant_dynamic-slice_fusion.3
  4.1 0.7 multiply_convert_fusion.wq_ref
  4.8 0.8 constant_dynamic-slice_fusion
  5.6 0.7 pad_maximum_fusion.wc_ref
  6.3 0.1 reshape_squeeze.3
  6.4 0.7 copy.12
  7.1 92.0 %shard_map.113 = (bf16[256,1024]{1,0:T(8,128)(2,1)}, f32[1,256]{1,0:T(1,128)}) custom-call(s32[4,256]{1,0:T(4,128)} %bitcast.5, bf16[256,768]{1,0:T(8,128)(2,1)} %bt_ref.1, bf16[48,128]{1,0:T(8,128)(2,1)} %pad_maximum_fusion.wc_ref, bf16[32,384]{1,0:T(8,128)(2,1)} %multiply_convert_fusion.wq_ref, bf16[32,1024]{1,0:T(8,128)(2,1)} %wo_ref.1, ...), custom_call_target="tpu_custom_call" | custom-call | tf_op jit(solution)/shard_map/pallas_call | solution.py:389
  99.1 0.0 copy-start.1
  99.1 1.9 %copy.15 = bf16[1,256,1024]{2,1,0:T(8,128)(2,1)} copy(bf16[1,256,1024]{2,1,0:T(8,128)(2,1)} %bitcast.4) | data formatting | bytes 1048576
  101.0 0.0 copy-done.1
  101.0 0.6 copy.16
Async XLA Ops:
  0.7 1.3 %copy-start = (s32[1,1024]{1,0:T(1,128)S(1)}, s32[1,1024]{1,0:T(1,128)}, u32[]{:S(2)}) copy-start(s32[1,1024]{1,0:T(1,128)} %param.10) | copy-start | bytes 12292
  99.1 1.9 %copy-start.1 = (f32[1,256]{1,0:T(1,128)S(1)}, f32[1,256]{1,0:T(1,128)}, u32[]{:S(2)}) copy-start(f32[1,256]{1,0:T(1,128)} %get-tuple-element.13) | copy-start | bytes 3076

commit v2 on v1

--- a/solution.py
+++ b/solution.py
@@ -41,41 +41,22 @@
 
 
 def kernel(
-    ids_ref, bt_ref, wc_ref, wq_ref, wo_ref, cos_ref, sin_ref, teach_ref, align_ref,
+    ids_ref, bt_ref, wconv_ref, wqkv_ref, wo_ref, gain_ref, cos_ref, sin_ref, teach_ref, align_ref,
     hid_ref, loss_ref,
-    ids_all, scale_all, wc_all, tt, wg, wo, ut, k_scr, vt_scr, qt_scr, lat_scr, att_out, att_in,
+    wc_src, wq_src, ids_all, scale_all, wc_all, tt, wg, wo, ut, k_scr, vt_scr, qt_scr, lat_scr, att_out, att_in,
+    gain_scr, hot, raw_kv, raw_q,
     ids_s, ids_r, sc_s, sc_r, wc_s, wc_r, ty_s, ty_r, t3_s, t3_r, t4_s, t4_r, t5_s, t5_r,
     wg_s, wg_r, wgx_s, wgx_r, wo_s, wo_r, wo2_s, wo2_r, wo3_s, wo3_r, at_s, at_r,
 ):
     f = lax.axis_index("fsdp")
     c = lax.axis_index("ctx")
-    g, core = f // 2, f % 2
+    core = f % 2
     y, zh = f // 4, (f // 2) % 2
     zl, x = c // 4, c % 4
     tap = f // 8
     sib = (f // 2) * 2 + 1 - core
     zfull = zh * 4 + zl
-
-    def same_core(i):
-        return (((g + i) % 16) * 2 + core, c)
-
-    def ctx_peer(i):
-        return (f, (c + i) % NCTX)
-
-    def mate(i):
-        return (tap * 8 + (f % 8 + i) % 8, c)
-
-    def z_dev(step):
-        z2 = (zfull + step + 8) % 8
-        return (y * 4 + (z2 // 4) * 2 + core, (z2 % 4) * 4 + x)
-
-    def x_dev(step):
-        return (f, zl * 4 + (x + step + 4) % 4)
-
-    barrier = pltpu.get_barrier_semaphore()
-
-    def sig(dev):
-        pl.semaphore_signal(barrier, inc=1, device_id=dev, device_id_type=MESH)
+    steps = (1, -1, 2)
 
     def loop(lo, hi, fn):
         def step(i, carry):
@@ -84,48 +65,145 @@
 
         lax.fori_loop(lo, hi, step, 0)
 
-    loop(1, 16, lambda i: sig(same_core(i)))
+    def ctx_peer(i):
+        return (f, (c + i) % NCTX)
+
+    def y_peer(i):
+        return (((y + i) % 8) * 4 + zh * 2 + core, c)
+
+    def mate_row(d):
+        return y - y % 2 + (y + d // 2) % 2
+
+    def block_dev(step, d):
+        z2 = (zfull + step + 8) % 8
+        return (mate_row(d) * 4 + (z2 // 4) * 2 + (core + d) % 2, (z2 % 4) * 4 + x)
+
+    def z_dev(step):
+        return block_dev(step, 0)
+
+    def x_dev(step):
+        return (f, zl * 4 + (x + step + 4) % 4)
+
+    barrier = pltpu.get_barrier_semaphore()
+
+    def sig(dev):
+        pl.semaphore_signal(barrier, inc=1, device_id=dev, device_id_type=MESH)
+
+    for d in range(4):
+        for step in (1, -1, 2, -2):
+            sig(block_dev(step, d))
+    for d in range(1, 4):
+        sig(block_dev(0, d))
+    loop(1, 8, lambda i: sig(y_peer(i)))
     loop(1, 16, lambda i: sig(ctx_peer(i)))
-    loop(1, 8, lambda i: sig(mate(i)))
-    sig((sib, c))
-    sig(z_dev(1))
-    sig(z_dev(-1))
-    sig(z_dev(-2))
-    pl.semaphore_wait(barrier, 15 + 15 + 7 + 1 + 3)
-
-    def wc_copy(i, slot):
-        return rc(wc_ref, wc_all.at[slot], wc_s.at[i], wc_r.at[i], mate(i))
-
-    loop(1, 8, lambda i: wc_copy(i, f % 8).start())
-    wc_all[f % 8] = wc_ref[...]
+
+    reach = jnp.where(zl == 3, 1, -1)
+    at_edge = (zl == 3) | (zl == 0)
+    gain_scr[...] = jnp.broadcast_to(
+        gain_ref[:, pl.ds(pl.multiple_of(f // 4 * 128, 128), 128)].astype(F32), (128, 128)
+    ).T
+    my_gain = gain_scr[pl.ds(pl.multiple_of(f % 4 * 32, 32), 32), 0:1]
+
+    def pack(slot, z):
+        col = z * 4 + x
+        both = wconv_ref[:, pl.ds(pl.multiple_of(col // 2 * 128, 128), 128)]
+        mine = jnp.where(col % 2 == 0, both[:, :64], both[:, 64:])
+        wc_src[slot] = jnp.concatenate([mine[:48], mine[48:]], axis=1)
+
+        def heads_of(start):
+            two = wqkv_ref[:, pl.ds(pl.multiple_of(start + z // 2 * 128, 128), 128)]
+            return jnp.where(z % 2 == 0, two[:, :64], two[:, 64:])
+
+        mine = jnp.concatenate(
+            [wqkv_ref[:, pl.ds(pl.multiple_of(z * 256, 256), 256)], heads_of(HQ * HD), heads_of((HQ + HK) * HD)],
+            axis=1,
+        )
+        wq_src[slot] = (mine.astype(F32) * my_gain).astype(BF16)
+
+    pack(0, zl)
+    for t in (1, 2):
+        pack(t, (zl + reach * t + 4) % 4)
+
+    def mate_slot(d, half_z):
+        return (y + d // 2) % 2 * 4 + half_z * 2 + (core + d) % 2
+
+    my_slot = mate_slot(0, zh)
+    wc_all[my_slot] = wc_src[0]
+    ids_all[c] = ids_ref[...]
+    wg[y * 2 + zh, core] = wq_src[0]
+
+    def quarter(z):
+        return jnp.where(core == 0, x, z)
+
+    def wo_cols(z):
+        return wo_ref.at[:, pl.ds(pl.multiple_of(quarter(z) * 256, 256), 256)]
+
+    my_quarter = quarter(zl)
+    wo[my_quarter, y * 2 + zh, core] = wo_ref[:, pl.ds(pl.multiple_of(my_quarter * 256, 256), 256)]
+    pl.semaphore_wait(barrier, 16 + 3 + 7 + 15)
+
+    def wc_copy(d, slot):
+        return rc(wc_src.at[0], wc_all.at[slot], wc_s.at[d], wc_r.at[d], block_dev(0, d))
+
+    def wc_near(t, d, slot):
+        return rc(
+            wc_src.at[t], wc_all.at[slot], wc_s.at[4 * t + d], wc_r.at[4 + d], block_dev(reach * t, d)
+        )
+
+    def wq_near(t, slot):
+        return rc(wq_src.at[t], wg.at[slot, core], wg_s.at[15 + t], wg_r.at[16], z_dev(reach * t))
+
+    def wo_near(t, slot):
+        z = (zl + reach * t + 4) % 4
+        return rc(wo_cols(z), wo.at[quarter(z), slot, core], wo_s.at[15 + t], wo_r.at[16], z_dev(reach * t))
+
+    @pl.when(at_edge)
+    def _():
+        for t in (1, 2):
+            for d in range(4):
+                wc_near(t, d, my_slot).start()
+
+    for d in range(1, 4):
+        wc_copy(d, my_slot).start()
+
+    @pl.when(at_edge)
+    def _():
+        for t in (1, 2):
+            wq_near(t, y * 2 + zh).start()
+            wo_near(t, y * 2 + zh).start()
 
     def ids_copy(i, slot):
         return rc(ids_ref, ids_all.at[slot], ids_s.at[i], ids_r.at[i], ctx_peer(i))
 
     loop(1, 16, lambda i: ids_copy(i, c).start())
-    ids_all[c] = ids_ref[...]
-
-    def wg_copy(i, slot):
-        return rc(wq_ref, wg.at[slot, core], wg_s.at[i], wg_r.at[i], same_core(i))
-
-    loop(1, 16, lambda i: wg_copy(i, g).start())
-    wg[g, core] = wq_ref[...]
+
+    def wg_copy(i, row, half_z):
+        ref = wg.at[row * 2 + half_z, core]
+        n = i + 8 * jnp.where(half_z == zh, 0, 1)
+        return rc(ref, ref, wg_s.at[n], wg_r.at[n], y_peer(i))
+
+    def wo_copy(i, row, half_z):
+        ref = wo.at[my_quarter, row * 2 + half_z, core]
+        n = i + 8 * jnp.where(half_z == zh, 0, 1)
+        return rc(ref, ref, wo_s.at[n], wo_r.at[n], y_peer(i))
+
+    loop(1, 8, lambda i: wg_copy(i, y, zh).start())
 
     btt = bt_ref[...].T
     bta = jnp.concatenate([btt[m * 96 : m * 96 + 48] for m in range(8)], axis=0)
     btb = jnp.concatenate([btt[m * 96 + 48 : m * 96 + 96] for m in range(8)], axis=0)
 
-    loop(1, 8, lambda i: wc_copy(i, (f % 8 - i + 8) % 8).wait_recv())
+    for d in range(1, 4):
+        wc_copy(d, mate_slot(d, zh)).wait_recv()
+    for d in range(4):
+        wc_near(1, d, mate_slot(d, 1 - zh)).wait_recv()
     wc_val = wc_all[...].reshape(384, 128)
     piece = tn(wc_val, bta)[:64] + tn(wc_val, btb)[64:]
     half = pl.ds(pl.multiple_of(core * 512, 512), 512)
 
-    def y_dev(step):
-        return (((y + 2 * step) % 8) * 4 + zh * 2 + core, c)
-
     def y_copy(step, from_tap):
         ref = tt.at[zl, x, :, pl.ds(pl.multiple_of(from_tap * 256, 256), 256)]
-        return rc(ref, ref, ty_s.at[step], ty_r.at[step], y_dev(step))
+        return rc(ref, ref, ty_s.at[step], ty_r.at[step], y_peer(2 * step))
 
     @pl.when(tap // 2 == core)
     def _():
@@ -133,6 +211,9 @@
         for step in (1, 2, 3):
             y_copy(step, tap).start()
 
+    wq_near(1, y * 2 + 1 - zh).wait_recv()
+    loop(1, 8, lambda i: wg_copy(i, y, 1 - zh).start())
+
     for step in (1, 2, 3):
         src_tap = (tap - step + 4) % 4
 
@@ -145,8 +226,6 @@
     def first_copy(n, dev, ref):
         return rc(ref, ref, t3_s.at[n], t3_r.at[n], dev)
 
-    steps = (1, -1, 2)
-
     @pl.when(core == 0)
     def _():
         for n, s in enumerate(steps):
@@ -167,17 +246,21 @@
             ref = tt.at[zl, :, :, half]
             rc(ref, ref, t4_s.at[n], t4_r.at[n], z_dev(s)).start()
 
-    loop(1, 16, lambda i: wg_copy(i, (g - i + 16) % 16).wait_recv())
-    rc(wg.at[:, core], wg.at[:, core], wgx_s.at[0], wgx_r.at[0], (sib, c)).start()
-
-    def wo_copy(i, slot):
-        return rc(
-            wo_ref.at[:, pl.ds(pl.multiple_of(x * 256, 256), 256)],
-            wo.at[x, slot, core], wo_s.at[i], wo_r.at[i], same_core(i),
-        )
-
-    loop(1, 16, lambda i: wo_copy(i, g).start())
-    wo[x, g, core] = wo_ref[:, pl.ds(pl.multiple_of(x * 256, 256), 256)]
+    loop(1, 8, lambda i: wo_copy(i, y, zh).start())
+    rc(
+        wo_cols(zl), wo.at[my_quarter, y * 2 + 1 - zh, core], wo_s.at[16], wo_r.at[16], z_dev(1)
+    ).wait_recv()
+    loop(1, 8, lambda i: wo_copy(i, y, 1 - zh).start())
+
+    def make_hot(b, carry):
+        rows = lax.broadcasted_iota(jnp.int32, (256, BLK), 0)
+        block = ids_all[b]
+        for k in range(KW):
+            hot[b, k * 256 : (k + 1) * 256] = (block[k : k + 1, :] == rows).astype(BF16)
+        return carry
+
+    loop(1, 16, lambda i: ids_copy(i, (c - i + NCTX) % NCTX).wait_recv())
+    lax.fori_loop(0, 13 + x, make_hot, 0)
 
     @pl.when(core == 0)
     def _():
@@ -205,15 +288,12 @@
             ref = tt.at[:, (x - s + 4) % 4, :, other]
             rc(ref, ref, t5_s.at[n], t5_r.at[n], (sib, c)).wait_recv()
 
-    def one_hot(b):
-        rows = lax.broadcasted_iota(jnp.int32, (256, BLK), 0)
-        block = ids_all[b]
-        return jnp.concatenate(
-            [(block[k : k + 1, :] == rows).astype(BF16) for k in range(KW)], axis=0
-        )
+    for half_z in (0, 1):
+        loop(1, 8, lambda i: wg_copy(i, (y - i + 8) % 8, half_z).wait_recv())
+    rc(wg.at[:, core], wg.at[:, core], wgx_s.at[0], wgx_r.at[0], (sib, c)).start()
 
     tall = tt[...].reshape(D, D)
-    latent = jnp.dot(tall, one_hot(c), preferred_element_type=F32).astype(BF16)
+    latent = jnp.dot(tall, hot[c], preferred_element_type=F32).astype(BF16)
     wide = latent.astype(F32)
     scale = lax.rsqrt(jnp.sum(wide * wide, axis=0, keepdims=True) * (1.0 / D) + norm_eps)
     scale_all[c] = scale
@@ -229,16 +309,33 @@
     rc(ref, ref, wgx_s.at[0], wgx_r.at[0], (sib, c)).wait_recv()
     ut[...] = tn(wg[...].reshape(D, 384), tall).astype(BF16)
 
-    loop(1, 16, lambda i: wo_copy(i, (g - i + 16) % 16).wait_recv())
-
-    def wo2_copy(n, s, slot):
+    for half_z in (0, 1):
+        loop(1, 8, lambda i: wo_copy(i, (y - i + 8) % 8, half_z).wait_recv())
+
+    def wo2_copy(n, dev, slot):
         ref = wo.at[slot, :, core]
-        return rc(ref, ref, wo2_s.at[n], wo2_r.at[n], x_dev(s))
-
-    for n, s in enumerate(steps):
-        wo2_copy(n, s, x).start()
-
-    loop(1, 16, lambda i: ids_copy(i, (c - i + NCTX) % NCTX).wait_recv())
+        return rc(ref, ref, wo2_s.at[n], wo2_r.at[n], dev)
+
+    @pl.when(core == 0)
+    def _():
+        for n, s in enumerate(steps):
+            wo2_copy(n, x_dev(s), my_quarter).start()
+
+    @pl.when(core == 1)
+    def _():
+        for n, s in enumerate(steps):
+            wo2_copy(n, z_dev(s), my_quarter).start()
+
+    def make_kv(b, carry):
+        raw_kv[b] = jnp.dot(ut[256:384, :], hot[b], preferred_element_type=F32)
+        return carry
+
+    def make_q(zb, carry):
+        raw_q[zb] = jnp.dot(ut[:256, :], hot[zb * 4 + x], preferred_element_type=F32)
+        return carry
+
+    lax.fori_loop(0, 13 + x, make_kv, 0)
+    lax.fori_loop(0, 4, make_q, 0)
     loop(1, 16, lambda i: sc_copy(i, (c - i + NCTX) % NCTX).wait_recv())
 
     def turn(v, b, scale_row):
@@ -247,25 +344,24 @@
         lo, hi = v[:32], v[32:]
         return jnp.concatenate([lo * cos - hi * sin, hi * cos + lo * sin], axis=0)
 
-    def make_kv(b, carry):
+    def turn_kv(b, carry):
         cols = pl.ds(pl.multiple_of(b * BLK, BLK), BLK)
-        kv = jnp.dot(ut[256:384, :], one_hot(b), preferred_element_type=F32)
-        k_scr[pl.ds(pl.multiple_of(b * BLK, BLK), BLK), :] = turn(kv[:64], b, scale_all[b]).T.astype(BF16)
-        vt_scr[:64, cols] = (kv[64:] * scale_all[b]).astype(BF16)
+        k_scr[pl.ds(pl.multiple_of(b * BLK, BLK), BLK), :] = (
+            turn(raw_kv[b, :64], b, scale_all[b]).astype(BF16).T
+        )
+        vt_scr[:64, cols] = (raw_kv[b, 64:] * scale_all[b]).astype(BF16)
         return carry
 
-    vt_scr[64:, :] = jnp.ones_like(vt_scr[64:, :])
-    lax.fori_loop(0, 13 + x, make_kv, 0)
-
-    def make_q(zb, carry):
+    def turn_q(zb, carry):
         b = zb * 4 + x
-        q = jnp.dot(ut[:256, :], one_hot(b), preferred_element_type=F32)
         row = scale_all[b] * (math.log2(math.e) / math.sqrt(HD))
         for h in range(4):
-            qt_scr[zb, :, h * BLK : (h + 1) * BLK] = turn(q[h * HD : (h + 1) * HD], b, row).astype(BF16)
+            qt_scr[zb, :, h * BLK : (h + 1) * BLK] = turn(raw_q[zb, h * HD : (h + 1) * HD], b, row).astype(BF16)
         return carry
 
-    lax.fori_loop(0, 4, make_q, 0)
+    vt_scr[64:, :] = jnp.ones_like(vt_scr[64:, :])
+    lax.fori_loop(0, 13 + x, turn_kv, 0)
+    lax.fori_loop(0, 4, turn_q, 0)
 
     def scores(zb, i, h):
         keys = k_scr[pl.ds(pl.multiple_of(i * BLK, BLK), BLK), :]
@@ -318,7 +414,7 @@
     lax.fori_loop(1, 4, other_block, 0)
 
     for n, s in enumerate(steps):
-        wo2_copy(n, s, (x - s + 4) % 4).wait_recv()
+        wo2_copy(n, x_dev(s), (my_quarter - s + 4) % 4).wait_recv()
     rc(wo.at[:, :, core], wo.at[:, :, core], wo3_s.at[0], wo3_r.at[0], (sib, c)).start()
 
     att_in[zl] = attend(zl)
@@ -341,11 +437,22 @@
         total = total + jnp.sum(diff * diff, axis=1, keepdims=True)
     loss_ref[...] = jnp.broadcast_to(total * (1.0 / D), (BLK, 128)).T[0:1, :]
 
-    loop(1, 8, lambda i: wc_copy(i, f % 8).wait_send())
+    for d in range(1, 4):
+        wc_copy(d, my_slot).wait_send()
+
+    @pl.when(at_edge)
+    def _():
+        for t in (1, 2):
+            for d in range(4):
+                wc_near(t, d, my_slot).wait_send()
+            wq_near(t, y * 2 + zh).wait_send()
+            wo_near(t, y * 2 + zh).wait_send()
+
     loop(1, 16, lambda i: ids_copy(i, c).wait_send())
-    loop(1, 16, lambda i: wg_copy(i, g).wait_send())
-    loop(1, 16, lambda i: wo_copy(i, g).wait_send())
     loop(1, 16, lambda i: sc_copy(i, c).wait_send())
+    for half_z in (0, 1):
+        loop(1, 8, lambda i: wg_copy(i, y, half_z).wait_send())
+        loop(1, 8, lambda i: wo_copy(i, y, half_z).wait_send())
 
     @pl.when(tap // 2 == core)
     def _():
@@ -356,7 +463,7 @@
         first_copy(n, z_dev(s), own).wait_send()
         ref = tt.at[:, x, :, half]
         rc(ref, ref, t4_s.at[n], t4_r.at[n], x_dev(s)).wait_send()
-        wo2_copy(n, s, x).wait_send()
+        wo2_copy(n, x_dev(s), my_quarter).wait_send()
     for n in range(4):
         ref = tt.at[:, x, :, half]
         rc(ref, ref, t5_s.at[n], t5_r.at[n], (sib, c)).wait_send()
@@ -367,22 +474,7 @@
 
 
 def body(byte_ids, byte_table, w_conv, w_qkv, w_out, norm_gain, teacher, align):
-    f = lax.axis_index("fsdp")
-    c = lax.axis_index("ctx")
-    zl = c // 4
     ids = byte_ids[0].reshape(BLK, KW).T
-    wc = lax.dynamic_slice_in_dim(w_conv, c * 64, 64, axis=1)
-    wc = jnp.concatenate([wc[:48], wc[48:]], axis=1)
-    wq = jnp.concatenate(
-        [
-            lax.dynamic_slice_in_dim(w_qkv, zl * 256, 256, axis=1),
-            lax.dynamic_slice_in_dim(w_qkv, HQ * HD + zl * HD, HD, axis=1),
-            lax.dynamic_slice_in_dim(w_qkv, (HQ + HK) * HD + zl * HD, HD, axis=1),
-        ],
-        axis=1,
-    )
-    gain = lax.dynamic_slice_in_dim(norm_gain, f * 32, 32, axis=0)
-    wq = (wq.astype(F32) * gain.astype(F32)[:, None]).astype(BF16)
     cos, sin = rope_tables(NCTX * BLK)
     vm = pl.BlockSpec(memory_space=pltpu.VMEM)
     dma = pltpu.SemaphoreType.DMA
@@ -392,9 +484,11 @@
             jax.ShapeDtypeStruct((BLK, D), BF16),
             jax.ShapeDtypeStruct((1, BLK), F32),
         ),
-        in_specs=[vm] * 9,
+        in_specs=[vm] * 10,
         out_specs=(vm, vm),
         scratch_shapes=[
+            pltpu.VMEM((3, 48, 128), BF16),
+            pltpu.VMEM((3, 32, 384), BF16),
             pltpu.VMEM((NCTX, KW, BLK), jnp.int32),
             pltpu.VMEM((NCTX, 1, BLK), F32),
             pltpu.VMEM((8, 48, 128), BF16),
@@ -408,15 +502,19 @@
             pltpu.VMEM((BLK, D), BF16),
             pltpu.VMEM((4, BLK, BLK), BF16),
             pltpu.VMEM((4, BLK, BLK), BF16),
+            pltpu.VMEM((128, 128), F32),
+            pltpu.VMEM((NCTX, D, BLK), BF16),
+            pltpu.VMEM((NCTX, 128, BLK), F32),
+            pltpu.VMEM((4, BLK, BLK), F32),
         ]
         + [
             dma((n,))
-            for n in (16, 16, 16, 16, 8, 8, 4, 4, 3, 3, 3, 3, 4, 4, 16, 16, 1, 1, 16, 16, 3, 3, 1, 1, 4, 4)
+            for n in (16, 16, 16, 16, 12, 8, 4, 4, 3, 3, 3, 3, 4, 4, 18, 17, 1, 1, 18, 17, 3, 3, 1, 1, 4, 4)
         ],
         compiler_params=pltpu.CompilerParams(
             collective_id=0, has_side_effects=True, vmem_limit_bytes=56 * 2**20
         ),
-    )(ids, byte_table, wc, wq, w_out, jnp.asarray(cos), jnp.asarray(sin), teacher[0], align)
+    )(ids, byte_table, w_conv, w_qkv, w_out, norm_gain[None], jnp.asarray(cos), jnp.asarray(sin), teacher[0], align)
     return hidden[None], loss
 
 

time: 102 us -> 84.8 us (0.83)
  the two profiles are of different devices: /device:TPU:63 before, /device:TPU:6 now
where the time goes in v2:
time: 84.8 us; the launch traced here: 84.6 us
  Pallas kernels  78.3 us (92%)
  local copies, waits for them, and re-layouts  4.34 us (5%)
  other arithmetic  1.36 us (2%)
    pallas_call x1, Pallas kernels, body(): pl.pallas_call(kernel, out_shape=(jax.ShapeDtypeStruct((BLK, D), BF16), j...  78.3 us
    unnamed x7, local copies, waits for them, and re-layouts  2.95 us

profile of v2, /device:TPU:6, one launch (start us, length us, event | category | flops | bytes accessed | tf_op | source)
XLA Modules:
  0.0 84.6 jit_solution(15516815418412016086)
XLA Ops:
  0.6 0.5 broadcast.3
  1.1 0.0 copy-start
  1.1 1.4 %reduce.3 = s32[1024]{0:T(1024)S(1)} reduce(s32[1,1024]{1,0:T(1,128)} %param.10, s32[]{:T(128)} %broadcast.3), dimensions={0}, to_apply=%param.10.reduce_sub_computation.3 | reduce | bytes 8196 | tf_op args[0]
  2.5 0.0 copy-done
  2.5 0.6 broadcast_in_dim.6.gain_ref
  3.1 0.1 reshape_squeeze.3
  3.2 0.7 copy.12
  3.9 78.3 %shard_map.113 = (bf16[256,1024]{1,0:T(8,128)(2,1)}, f32[1,256]{1,0:T(1,128)}) custom-call(s32[4,256]{1,0:T(4,128)} %bitcast.5, bf16[256,768]{1,0:T(8,128)(2,1)} %bt_ref.1, bf16[96,1024]{1,0:T(8,128)(2,1)} %wconv_ref.1, bf16[32,1536]{1,0:T(8,128)(2,1)} %wqkv_ref.1, bf16[32,1024]{1,0:T(8,128)(2,1)} %wo_ref.1, bf16[1,1024]{1,0:T(2,128)(2,1)} %broadcast_in_dim.6.gain_ref, ...), custom_call_target="tpu_custom_call" | custom-call | tf_op jit(solution)/shard_map/pallas_call | solution.py:481
  82.2 0.0 copy-start.1
  82.2 1.9 %copy.15 = bf16[1,256,1024]{2,1,0:T(8,128)(2,1)} copy(bf16[1,256,1024]{2,1,0:T(8,128)(2,1)} %bitcast.3) | data formatting | bytes 1048576
  84.1 0.0 copy-done.1
  84.1 0.6 copy.16
Async XLA Ops:
  1.1 1.4 %copy-start = (bf16[1024]{0:T(1024)(128)(2,1)S(1)}, bf16[1024]{0:T(1024)(128)(2,1)}, u32[]{:S(2)}) copy-start(bf16[1024]{0:T(1024)(128)(2,1)} %param.15) | copy-start | bytes 6148
  82.2 1.9 %copy-start.1 = (f32[1,256]{1,0:T(1,128)S(1)}, f32[1,256]{1,0:T(1,128)}, u32[]{:S(2)}) copy-start(f32[1,256]{1,0:T(1,128)} %get-tuple-element.9) | copy-start | bytes 3076

commit v3 on v2

--- a/solution.py
+++ b/solution.py
@@ -41,10 +41,10 @@
 
 
 def kernel(
-    ids_ref, bt_ref, wconv_ref, wqkv_ref, wo_ref, gain_ref, cos_ref, sin_ref, teach_ref, align_ref,
+    ids_ref, bt_ref, wconv_ref, wqkv_ref, wo_ref, gain_ref, cos_hbm, sin_hbm, teach_hbm, align_ref,
     hid_ref, loss_ref,
     wc_src, wq_src, ids_all, scale_all, wc_all, tt, wg, wo, ut, k_scr, vt_scr, qt_scr, lat_scr, att_out, att_in,
-    gain_scr, hot, raw_kv, raw_q,
+    gain_scr, hot, raw_kv, raw_q, lat_acc, cos_ref, sin_ref, teach_ref, in_s,
     ids_s, ids_r, sc_s, sc_r, wc_s, wc_r, ty_s, ty_r, t3_s, t3_r, t4_s, t4_r, t5_s, t5_r,
     wg_s, wg_r, wgx_s, wgx_r, wo_s, wo_r, wo2_s, wo2_r, wo3_s, wo3_r, at_s, at_r,
 ):
@@ -99,17 +99,66 @@
 
     reach = jnp.where(zl == 3, 1, -1)
     at_edge = (zl == 3) | (zl == 0)
-    gain_scr[...] = jnp.broadcast_to(
-        gain_ref[:, pl.ds(pl.multiple_of(f // 4 * 128, 128), 128)].astype(F32), (128, 128)
-    ).T
-    my_gain = gain_scr[pl.ds(pl.multiple_of(f % 4 * 32, 32), 32), 0:1]
-
-    def pack(slot, z):
+
+    def pack_conv(slot, z):
         col = z * 4 + x
         both = wconv_ref[:, pl.ds(pl.multiple_of(col // 2 * 128, 128), 128)]
         mine = jnp.where(col % 2 == 0, both[:, :64], both[:, 64:])
         wc_src[slot] = jnp.concatenate([mine[:48], mine[48:]], axis=1)
 
+    def mate_slot(d, half_z):
+        return (y + d // 2) % 2 * 4 + half_z * 2 + (core + d) % 2
+
+    my_slot = mate_slot(0, zh)
+    pack_conv(0, zl)
+    for t in (1, 2):
+        pack_conv(t, (zl + reach * t + 4) % 4)
+    wc_all[my_slot] = wc_src[0]
+    pl.semaphore_wait(barrier, 16 + 3 + 7 + 15)
+
+    def wc_copy(d, slot):
+        return rc(wc_src.at[0], wc_all.at[slot], wc_s.at[d], wc_r.at[d], block_dev(0, d))
+
+    def wc_near(t, d, slot):
+        return rc(
+            wc_src.at[t], wc_all.at[slot], wc_s.at[4 * t + d], wc_r.at[4 + d], block_dev(reach * t, d)
+        )
+
+    @pl.when(at_edge)
+    def _():
+        for t in (1, 2):
+            for d in range(4):
+                wc_near(t, d, my_slot).start()
+
+    for d in range(1, 4):
+        wc_copy(d, my_slot).start()
+
+    late = [
+        pltpu.make_async_copy(src, dst, in_s.at[n])
+        for n, (src, dst) in enumerate(((cos_hbm, cos_ref), (sin_hbm, sin_ref), (teach_hbm, teach_ref)))
+    ]
+    for copy in late:
+        copy.start()
+
+    taps = lax.broadcasted_iota(jnp.int32, (8, 4 * BLK), 0)
+    at = lax.broadcasted_iota(jnp.int32, (8, 4 * BLK), 1)
+    spread = jnp.where(at % KW == taps, jnp.broadcast_to(ids_ref[...], (8, 4 * BLK)).astype(F32), 0.0)
+    to_row = lax.broadcasted_iota(jnp.int32, (4 * BLK, BLK), 0) // KW
+    to_row = (to_row == lax.broadcasted_iota(jnp.int32, (4 * BLK, BLK), 1)).astype(BF16)
+    rows_of = jnp.dot(spread.astype(BF16), to_row, preferred_element_type=F32)
+    ids_all[c] = rows_of[:KW].astype(jnp.int32)
+
+    def ids_copy(i, slot):
+        ref = ids_all.at[slot]
+        return rc(ref, ref, ids_s.at[i], ids_r.at[i], ctx_peer(i))
+
+    gains = gain_ref[...].astype(F32)
+    here = lax.broadcasted_iota(jnp.int32, (8, 128), 0) == f // 4
+    gains = jnp.sum(jnp.where(here, gains, 0.0), axis=0, keepdims=True)
+    gain_scr[...] = jnp.broadcast_to(gains, (128, 128)).T
+    my_gain = gain_scr[pl.ds(pl.multiple_of(f % 4 * 32, 32), 32), 0:1]
+
+    def pack_heads(slot, z):
         def heads_of(start):
             two = wqkv_ref[:, pl.ds(pl.multiple_of(start + z // 2 * 128, 128), 128)]
             return jnp.where(z % 2 == 0, two[:, :64], two[:, 64:])
@@ -120,16 +169,9 @@
         )
         wq_src[slot] = (mine.astype(F32) * my_gain).astype(BF16)
 
-    pack(0, zl)
+    pack_heads(0, zl)
     for t in (1, 2):
-        pack(t, (zl + reach * t + 4) % 4)
-
-    def mate_slot(d, half_z):
-        return (y + d // 2) % 2 * 4 + half_z * 2 + (core + d) % 2
-
-    my_slot = mate_slot(0, zh)
-    wc_all[my_slot] = wc_src[0]
-    ids_all[c] = ids_ref[...]
+        pack_heads(t, (zl + reach * t + 4) % 4)
     wg[y * 2 + zh, core] = wq_src[0]
 
     def quarter(z):
@@ -140,15 +182,6 @@
 
     my_quarter = quarter(zl)
     wo[my_quarter, y * 2 + zh, core] = wo_ref[:, pl.ds(pl.multiple_of(my_quarter * 256, 256), 256)]
-    pl.semaphore_wait(barrier, 16 + 3 + 7 + 15)
-
-    def wc_copy(d, slot):
-        return rc(wc_src.at[0], wc_all.at[slot], wc_s.at[d], wc_r.at[d], block_dev(0, d))
-
-    def wc_near(t, d, slot):
-        return rc(
-            wc_src.at[t], wc_all.at[slot], wc_s.at[4 * t + d], wc_r.at[4 + d], block_dev(reach * t, d)
-        )
 
     def wq_near(t, slot):
         return rc(wq_src.at[t], wg.at[slot, core], wg_s.at[15 + t], wg_r.at[16], z_dev(reach * t))
@@ -160,20 +193,8 @@
     @pl.when(at_edge)
     def _():
         for t in (1, 2):
-            for d in range(4):
-                wc_near(t, d, my_slot).start()
-
-    for d in range(1, 4):
-        wc_copy(d, my_slot).start()
-
-    @pl.when(at_edge)
-    def _():
-        for t in (1, 2):
             wq_near(t, y * 2 + zh).start()
             wo_near(t, y * 2 + zh).start()
-
-    def ids_copy(i, slot):
-        return rc(ids_ref, ids_all.at[slot], ids_s.at[i], ids_r.at[i], ctx_peer(i))
 
     loop(1, 16, lambda i: ids_copy(i, c).start())
 
@@ -199,15 +220,16 @@
         wc_near(1, d, mate_slot(d, 1 - zh)).wait_recv()
     wc_val = wc_all[...].reshape(384, 128)
     piece = tn(wc_val, bta)[:64] + tn(wc_val, btb)[64:]
-    half = pl.ds(pl.multiple_of(core * 512, 512), 512)
+
+    away = jnp.where(y % 2 == 0, -1, 1)
 
     def y_copy(step, from_tap):
-        ref = tt.at[zl, x, :, pl.ds(pl.multiple_of(from_tap * 256, 256), 256)]
-        return rc(ref, ref, ty_s.at[step], ty_r.at[step], y_peer(2 * step))
+        ref = tt.at[core, zl, x, :, pl.ds(pl.multiple_of(from_tap % 2 * 256, 256), 256)]
+        return rc(ref, ref, ty_s.at[step], ty_r.at[step], y_peer(8 + away * step))
 
     @pl.when(tap // 2 == core)
     def _():
-        tt[zl, x, :, pl.ds(pl.multiple_of(tap * 256, 256), 256)] = piece.astype(BF16)
+        tt[core, zl, x, :, pl.ds(pl.multiple_of(tap % 2 * 256, 256), 256)] = piece.astype(BF16)
         for step in (1, 2, 3):
             y_copy(step, tap).start()
 
@@ -215,36 +237,68 @@
     loop(1, 8, lambda i: wg_copy(i, y, 1 - zh).start())
 
     for step in (1, 2, 3):
-        src_tap = (tap - step + 4) % 4
+        src_tap = (tap + (away, -away, 2)[step - 1] + 4) % 4
 
         @pl.when(src_tap // 2 == core)
         def _():
             y_copy(step, src_tap).wait_recv()
 
-    own = tt.at[zl, x, :, half]
+    own = tt.at[core, zl, x]
 
     def first_copy(n, dev, ref):
         return rc(ref, ref, t3_s.at[n], t3_r.at[n], dev)
+
+    ways = (1, -1, 1, -1, 1, -1)
+    parts = (0, 2, 2, 0, 0, 2)
+
+    def along_x(n, shift):
+        ref = tt.at[core, pl.ds(parts[n], 2), (x + shift + 4) % 4]
+        return rc(ref, ref, t4_s.at[n], t4_r.at[n], x_dev(ways[n]))
+
+    def along_z(n, shift):
+        ref = tt.at[core, (zl + shift + 4) % 4, pl.ds(parts[n], 2)]
+        return rc(ref, ref, t4_s.at[n], t4_r.at[n], z_dev(ways[n]))
+
+    def over(n, ref):
+        return rc(ref, ref, t5_s.at[n], t5_r.at[n], (sib, c))
+
+    def second_axis(along, slice_of):
+        over(0, slice_of(0, core)).start()
+        along(0, -1).wait_recv()
+        along(4, -1).start()
+        along(1, 1).wait_recv()
+        along(5, 1).start()
+        along(2, -1).wait_recv()
+        over(1, slice_of(-1, core)).start()
+        along(3, 1).wait_recv()
+        over(2, slice_of(1, core)).start()
+        along(4, -2).wait_recv()
+        along(5, 2).wait_recv()
+        over(3, slice_of(2, core)).start()
+
+    def slice_x(shift, part):
+        return tt.at[part, :, (x + shift + 4) % 4]
+
+    def slice_z(shift, part):
+        return tt.at[part, (zl + shift + 4) % 4]
 
     @pl.when(core == 0)
     def _():
         for n, s in enumerate(steps):
             first_copy(n, z_dev(s), own).start()
         for n, s in enumerate(steps):
-            first_copy(n, z_dev(s), tt.at[(zl - s + 4) % 4, x, :, half]).wait_recv()
-        for n, s in enumerate(steps):
-            ref = tt.at[:, x, :, half]
-            rc(ref, ref, t4_s.at[n], t4_r.at[n], x_dev(s)).start()
+            first_copy(n, z_dev(s), tt.at[core, (zl - s + 4) % 4, x]).wait_recv()
+        for n in (0, 1, 2, 3):
+            along_x(n, 0).start()
 
     @pl.when(core == 1)
     def _():
         for n, s in enumerate(steps):
             first_copy(n, x_dev(s), own).start()
         for n, s in enumerate(steps):
-            first_copy(n, x_dev(s), tt.at[zl, (x - s + 4) % 4, :, half]).wait_recv()
-        for n, s in enumerate(steps):
-            ref = tt.at[zl, :, :, half]
-            rc(ref, ref, t4_s.at[n], t4_r.at[n], z_dev(s)).start()
+            first_copy(n, x_dev(s), tt.at[core, zl, (x - s + 4) % 4]).wait_recv()
+        for n in (0, 1, 2, 3):
+            along_z(n, 0).start()
 
     loop(1, 8, lambda i: wo_copy(i, y, zh).start())
     rc(
@@ -260,40 +314,40 @@
         return carry
 
     loop(1, 16, lambda i: ids_copy(i, (c - i + NCTX) % NCTX).wait_recv())
-    lax.fori_loop(0, 13 + x, make_hot, 0)
+    lax.fori_loop(0, NCTX, make_hot, 0)
 
     @pl.when(core == 0)
     def _():
-        ref = tt.at[:, x, :, half]
-        rc(ref, ref, t5_s.at[0], t5_r.at[0], (sib, c)).start()
-        for n, s in enumerate(steps):
-            ref = tt.at[:, (x - s + 4) % 4, :, half]
-            rc(ref, ref, t4_s.at[n], t4_r.at[n], x_dev(s)).wait_recv()
-            rc(ref, ref, t5_s.at[n + 1], t5_r.at[n + 1], (sib, c)).start()
-        other = pl.ds(512, 512)
-        for n, s in enumerate((0,) + steps):
-            ref = tt.at[(zl - s + 4) % 4, :, :, other]
-            rc(ref, ref, t5_s.at[n], t5_r.at[n], (sib, c)).wait_recv()
+        second_axis(along_x, slice_x)
 
     @pl.when(core == 1)
     def _():
-        ref = tt.at[zl, :, :, half]
-        rc(ref, ref, t5_s.at[0], t5_r.at[0], (sib, c)).start()
-        for n, s in enumerate(steps):
-            ref = tt.at[(zl - s + 4) % 4, :, :, half]
-            rc(ref, ref, t4_s.at[n], t4_r.at[n], z_dev(s)).wait_recv()
-            rc(ref, ref, t5_s.at[n + 1], t5_r.at[n + 1], (sib, c)).start()
-        other = pl.ds(0, 512)
-        for n, s in enumerate((0,) + steps):
-            ref = tt.at[:, (x - s + 4) % 4, :, other]
-            rc(ref, ref, t5_s.at[n], t5_r.at[n], (sib, c)).wait_recv()
+        second_axis(along_z, slice_z)
 
     for half_z in (0, 1):
         loop(1, 8, lambda i: wg_copy(i, (y - i + 8) % 8, half_z).wait_recv())
     rc(wg.at[:, core], wg.at[:, core], wgx_s.at[0], wgx_r.at[0], (sib, c)).start()
 
-    tall = tt[...].reshape(D, D)
-    latent = jnp.dot(tall, hot[c], preferred_element_type=F32).astype(BF16)
+    def table(part):
+        return tt[part].reshape(D, 512)
+
+    def hot_rows(b, part):
+        return hot[b, pl.ds(pl.multiple_of(part * 512, 512), 512)]
+
+    lat_acc[...] = jnp.dot(table(core), hot_rows(c, core), preferred_element_type=F32)
+
+    @pl.when(core == 0)
+    def _():
+        for n, shift in enumerate((0, -1, 1, 2)):
+            over(n, slice_z(shift, 1 - core)).wait_recv()
+
+    @pl.when(core == 1)
+    def _():
+        for n, shift in enumerate((0, -1, 1, 2)):
+            over(n, slice_x(shift, 1 - core)).wait_recv()
+
+    latent = lat_acc[...] + jnp.dot(table(1 - core), hot_rows(c, 1 - core), preferred_element_type=F32)
+    latent = latent.astype(BF16)
     wide = latent.astype(F32)
     scale = lax.rsqrt(jnp.sum(wide * wide, axis=0, keepdims=True) * (1.0 / D) + norm_eps)
     scale_all[c] = scale
@@ -307,7 +361,9 @@
 
     ref = wg.at[:, 1 - core]
     rc(ref, ref, wgx_s.at[0], wgx_r.at[0], (sib, c)).wait_recv()
-    ut[...] = tn(wg[...].reshape(D, 384), tall).astype(BF16)
+    wgt = wg[...].reshape(D, 384)
+    for part in (0, 1):
+        ut[:, part * 512 : (part + 1) * 512] = tn(wgt, table(part)).astype(BF16)
 
     for half_z in (0, 1):
         loop(1, 8, lambda i: wo_copy(i, (y - i + 8) % 8, half_z).wait_recv())
@@ -334,7 +390,7 @@
         raw_q[zb] = jnp.dot(ut[:256, :], hot[zb * 4 + x], preferred_element_type=F32)
         return carry
 
-    lax.fori_loop(0, 13 + x, make_kv, 0)
+    lax.fori_loop(0, NCTX, make_kv, 0)
     lax.fori_loop(0, 4, make_q, 0)
     loop(1, 16, lambda i: sc_copy(i, (c - i + NCTX) % NCTX).wait_recv())
 
@@ -360,7 +416,9 @@
         return carry
 
     vt_scr[64:, :] = jnp.ones_like(vt_scr[64:, :])
-    lax.fori_loop(0, 13 + x, turn_kv, 0)
+    for copy in late:
+        copy.wait()
+    lax.fori_loop(0, NCTX, turn_kv, 0)
     lax.fori_loop(0, 4, turn_q, 0)
 
     def scores(zb, i, h):
@@ -375,17 +433,25 @@
         acc = acc * jnp.exp2(top - new_top) + jnp.dot(values, probs, preferred_element_type=F32)
         return new_top, acc
 
+    key_row = lax.broadcasted_iota(jnp.int32, (BLK, BLK), 0)
+    query_row = lax.broadcasted_iota(jnp.int32, (BLK, BLK), 1) + x * BLK
+
     def attend(zb):
-        n = zb * 4 + x
-
-        def one(i, carry):
+        def one(i, carry, masked_block):
             states, now = carry
-            later = [scores(zb, i + 1, h) for h in range(4)]
-            return [soft(i, now[h], states[h]) for h in range(4)], later
+            later, new_states = [], []
+            for h in range(4):
+                if masked_block != 3:
+                    later.append(scores(zb, i + 1, h))
+                s = now[h]
+                if masked_block is not None:
+                    s = jnp.where(key_row + masked_block * BLK <= query_row, s, masked_score)
+                new_states.append(soft(i, s, states[h]))
+            return new_states, later
 
         def four(j, carry):
             for k in range(4):
-                carry = one(j * 4 + k, carry)
+                carry = one(j * 4 + k, carry, None)
             return carry
 
         carry = (
@@ -393,37 +459,44 @@
             [scores(zb, 0, h) for h in range(4)],
         )
         carry = lax.fori_loop(0, zb, four, carry)
-        states, now = lax.fori_loop(4 * zb, n, one, carry)
-        rows = lax.broadcasted_iota(jnp.int32, (BLK, BLK), 0)
-        cols = lax.broadcasted_iota(jnp.int32, (BLK, BLK), 1)
-        outs = []
+        for k in range(4):
+            carry = one(4 * zb + k, carry, k)
         for h in range(4):
-            _, acc = soft(n, jnp.where(rows <= cols, now[h], masked_score), states[h])
-            outs.append((acc[:HD] / acc[HD : HD + 1]).astype(BF16))
-        return jnp.concatenate(outs, axis=0)
-
-    def att_copy(i, zb, slot):
-        return rc(att_out.at[i], att_in.at[slot], at_s.at[i], at_r.at[i], (f, zb * 4 + x))
-
-    def other_block(i, carry):
+            _, acc = carry[0][h]
+            att_out[zb, h * HD : (h + 1) * HD] = (acc[:HD] / acc[HD : HD + 1]).astype(BF16)
+
+    def att_copy(zb, slot):
+        return rc(att_out.at[zb], att_in.at[slot], at_s.at[zb], at_r.at[slot], (f, zb * 4 + x))
+
+    def block_step(i, carry):
         zb = (zl + i) % 4
-        att_out[i] = attend(zb)
-        att_copy(i, zb, zl).start()
+
+        @pl.when(i == 3)
+        def _():
+            for n, s in enumerate(steps):
+                wo2_copy(n, x_dev(s), (my_quarter - s + 4) % 4).wait_recv()
+            rc(wo.at[:, :, core], wo.at[:, :, core], wo3_s.at[0], wo3_r.at[0], (sib, c)).start()
+
+        for k in range(4):
+
+            @pl.when(zb == k)
+            def _():
+                attend(k)
+
+        @pl.when(i < 4)
+        def _():
+            att_copy(zb, zl).start()
+
         return carry
 
-    lax.fori_loop(1, 4, other_block, 0)
-
-    for n, s in enumerate(steps):
-        wo2_copy(n, x_dev(s), (my_quarter - s + 4) % 4).wait_recv()
-    rc(wo.at[:, :, core], wo.at[:, :, core], wo3_s.at[0], wo3_r.at[0], (sib, c)).start()
-
-    att_in[zl] = attend(zl)
+    lax.fori_loop(1, 5, block_step, 0)
+    att_in[zl] = att_out[zl]
 
     ref = wo.at[:, :, 1 - core]
     rc(ref, ref, wo3_s.at[0], wo3_r.at[0], (sib, c)).wait_recv()
     for i in (1, 2, 3):
         slot = (zl - i + 4) % 4
-        att_copy(i, slot, slot).wait_recv()
+        att_copy(slot, slot).wait_recv()
 
     attended = att_in[...].reshape(D, BLK)
     pick = (align_ref[...] - c * BLK == lax.broadcasted_iota(jnp.int32, (BLK, BLK), 0)).astype(BF16)
@@ -461,20 +534,18 @@
 
     for n, s in enumerate(steps):
         first_copy(n, z_dev(s), own).wait_send()
-        ref = tt.at[:, x, :, half]
-        rc(ref, ref, t4_s.at[n], t4_r.at[n], x_dev(s)).wait_send()
         wo2_copy(n, x_dev(s), my_quarter).wait_send()
+    for n in range(6):
+        along_x(n, 0).wait_send()
     for n in range(4):
-        ref = tt.at[:, x, :, half]
-        rc(ref, ref, t5_s.at[n], t5_r.at[n], (sib, c)).wait_send()
+        over(n, slice_x(0, core)).wait_send()
     rc(wg.at[:, core], wg.at[:, core], wgx_s.at[0], wgx_r.at[0], (sib, c)).wait_send()
     rc(wo.at[:, :, core], wo.at[:, :, core], wo3_s.at[0], wo3_r.at[0], (sib, c)).wait_send()
     for i in (1, 2, 3):
-        att_copy(i, zl, zl).wait_send()
+        att_copy((zl + i) % 4, zl).wait_send()
 
 
 def body(byte_ids, byte_table, w_conv, w_qkv, w_out, norm_gain, teacher, align):
-    ids = byte_ids[0].reshape(BLK, KW).T
     cos, sin = rope_tables(NCTX * BLK)
     vm = pl.BlockSpec(memory_space=pltpu.VMEM)
     dma = pltpu.SemaphoreType.DMA
@@ -484,7 +555,7 @@
             jax.ShapeDtypeStruct((BLK, D), BF16),
             jax.ShapeDtypeStruct((1, BLK), F32),
         ),
-        in_specs=[vm] * 10,
+        in_specs=[vm] * 6 + [pl.BlockSpec(memory_space=pl.ANY)] * 3 + [vm],
         out_specs=(vm, vm),
         scratch_shapes=[
             pltpu.VMEM((3, 48, 128), BF16),
@@ -492,7 +563,7 @@
             pltpu.VMEM((NCTX, KW, BLK), jnp.int32),
             pltpu.VMEM((NCTX, 1, BLK), F32),
             pltpu.VMEM((8, 48, 128), BF16),
-            pltpu.VMEM((4, 4, 64, 1024), BF16),
+            pltpu.VMEM((2, 4, 4, 64, 512), BF16),
             pltpu.VMEM((16, 2, 32, 384), BF16),
             pltpu.VMEM((4, 16, 2, 32, 256), BF16),
             pltpu.VMEM((384, 1024), BF16),
@@ -506,15 +577,20 @@
             pltpu.VMEM((NCTX, D, BLK), BF16),
             pltpu.VMEM((NCTX, 128, BLK), F32),
             pltpu.VMEM((4, BLK, BLK), F32),
+            pltpu.VMEM((D, BLK), F32),
+            pltpu.VMEM((HD // 2, NCTX * BLK), F32),
+            pltpu.VMEM((HD // 2, NCTX * BLK), F32),
+            pltpu.VMEM((BLK, D), BF16),
+            pltpu.SemaphoreType.DMA((3,)),
         ]
         + [
             dma((n,))
-            for n in (16, 16, 16, 16, 12, 8, 4, 4, 3, 3, 3, 3, 4, 4, 18, 17, 1, 1, 18, 17, 3, 3, 1, 1, 4, 4)
+            for n in (16, 16, 16, 16, 12, 8, 4, 4, 3, 3, 6, 6, 4, 4, 18, 17, 1, 1, 18, 17, 3, 3, 1, 1, 4, 4)
         ],
         compiler_params=pltpu.CompilerParams(
             collective_id=0, has_side_effects=True, vmem_limit_bytes=56 * 2**20
         ),
-    )(ids, byte_table, w_conv, w_qkv, w_out, norm_gain[None], jnp.asarray(cos), jnp.asarray(sin), teacher[0], align)
+    )(byte_ids, byte_table, w_conv, w_qkv, w_out, norm_gain.reshape(8, 128), jnp.asarray(cos), jnp.asarray(sin), teacher[0], align)
     return hidden[None], loss
 
 

time: 84.8 us -> 77.8 us (0.917)
  the two profiles are of different devices: /device:TPU:6 before, /device:TPU:43 now
where the time goes in v3:
time: 77.8 us; the launch traced here: 77.7 us
  Pallas kernels  74.6 us (96%)
  local copies, waits for them, and re-layouts  2.44 us (3%)
    pallas_call x1, Pallas kernels, body(): pl.pallas_call(kernel, out_shape=(jax.ShapeDtypeStruct((BLK, D), BF16), j...  74.6 us
    unnamed x4, local copies, waits for them, and re-layouts  2.44 us

profile of v3, /device:TPU:43, one launch (start us, length us, event | category | flops | bytes accessed | tf_op | source)
XLA Modules:
  0.0 77.7 jit_solution(6415305968365696591)
XLA Ops:
  0.6 74.6 %shard_map.113 = (bf16[256,1024]{1,0:T(8,128)(2,1)}, f32[1,256]{1,0:T(1,128)}) custom-call(s32[1,1024]{1,0:T(1,128)} %ids_ref.1, bf16[256,768]{1,0:T(8,128)(2,1)} %bt_ref.1, bf16[96,1024]{1,0:T(8,128)(2,1)} %wconv_ref.1, bf16[32,1536]{1,0:T(8,128)(2,1)} %wqkv_ref.1, bf16[32,1024]{1,0:T(8,128)(2,1)} %wo_ref.1, bf16[8,128]{1,0:T(8,128)(2,1)} %bitcast.5, ...), custom_call_target="tpu_custom_call" | custom-call | tf_op jit(solution)/shard_map/pallas_call | solution.py:552
  75.2 0.0 copy-start
  75.2 1.9 %copy.14 = bf16[1,256,1024]{2,1,0:T(8,128)(2,1)} copy(bf16[1,256,1024]{2,1,0:T(8,128)(2,1)} %bitcast.4) | data formatting | bytes 1048576
  77.1 0.0 copy-done
  77.1 0.6 copy.15
Async XLA Ops:
  75.2 1.9 %copy-start = (f32[1,256]{1,0:T(1,128)S(1)}, f32[1,256]{1,0:T(1,128)}, u32[]{:S(2)}) copy-start(f32[1,256]{1,0:T(1,128)} %get-tuple-element.9) | copy-start | bytes 3076

commit v4 on v3

--- a/solution.py
+++ b/solution.py
@@ -259,6 +259,41 @@
         ref = tt.at[core, (zl + shift + 4) % 4, pl.ds(parts[n], 2)]
         return rc(ref, ref, t4_s.at[n], t4_r.at[n], z_dev(ways[n]))
 
+    def make_hot(b, carry):
+        rows = lax.broadcasted_iota(jnp.int32, (256, BLK), 0)
+        block = ids_all[b]
+        for k in range(KW):
+            hot[b, k * 256 : (k + 1) * 256] = (block[k : k + 1, :] == rows).astype(BF16)
+        return carry
+
+    def meanwhile():
+        loop(1, 8, lambda i: wo_copy(i, y, zh).start())
+        rc(
+            wo_cols(zl), wo.at[my_quarter, y * 2 + 1 - zh, core], wo_s.at[16], wo_r.at[16], z_dev(1)
+        ).wait_recv()
+        loop(1, 8, lambda i: wo_copy(i, y, 1 - zh).start())
+
+        loop(1, 16, lambda i: ids_copy(i, (c - i + NCTX) % NCTX).wait_recv())
+        lax.fori_loop(0, NCTX, make_hot, 0)
+        for d in range(1, 4):
+            wc_copy(d, my_slot).wait_send()
+
+        @pl.when(at_edge)
+        def _():
+            for t in (1, 2):
+                for d in range(4):
+                    wc_near(t, d, my_slot).wait_send()
+
+        loop(1, 16, lambda i: ids_copy(i, c).wait_send())
+
+        @pl.when(tap // 2 == core)
+        def _():
+            for step in (1, 2, 3):
+                y_copy(step, tap).wait_send()
+
+        for n, s in enumerate(steps):
+            first_copy(n, z_dev(s), own).wait_send()
+
     def over(n, ref):
         return rc(ref, ref, t5_s.at[n], t5_r.at[n], (sib, c))
 
@@ -268,6 +303,7 @@
         along(4, -1).start()
         along(1, 1).wait_recv()
         along(5, 1).start()
+        meanwhile()
         along(2, -1).wait_recv()
         over(1, slice_of(-1, core)).start()
         along(3, 1).wait_recv()
@@ -300,22 +336,6 @@
         for n in (0, 1, 2, 3):
             along_z(n, 0).start()
 
-    loop(1, 8, lambda i: wo_copy(i, y, zh).start())
-    rc(
-        wo_cols(zl), wo.at[my_quarter, y * 2 + 1 - zh, core], wo_s.at[16], wo_r.at[16], z_dev(1)
-    ).wait_recv()
-    loop(1, 8, lambda i: wo_copy(i, y, 1 - zh).start())
-
-    def make_hot(b, carry):
-        rows = lax.broadcasted_iota(jnp.int32, (256, BLK), 0)
-        block = ids_all[b]
-        for k in range(KW):
-            hot[b, k * 256 : (k + 1) * 256] = (block[k : k + 1, :] == rows).astype(BF16)
-        return carry
-
-    loop(1, 16, lambda i: ids_copy(i, (c - i + NCTX) % NCTX).wait_recv())
-    lax.fori_loop(0, NCTX, make_hot, 0)
-
     @pl.when(core == 0)
     def _():
         second_axis(along_x, slice_x)
@@ -365,6 +385,17 @@
     for part in (0, 1):
         ut[:, part * 512 : (part + 1) * 512] = tn(wgt, table(part)).astype(BF16)
 
+    def make_kv(b, carry):
+        raw_kv[b] = jnp.dot(ut[256:384, :], hot[b], preferred_element_type=F32)
+        return carry
+
+    def make_q(zb, carry):
+        raw_q[zb] = jnp.dot(ut[:256, :], hot[zb * 4 + x], preferred_element_type=F32)
+        return carry
+
+    lax.fori_loop(0, NCTX, make_kv, 0)
+    lax.fori_loop(0, 4, make_q, 0)
+
     for half_z in (0, 1):
         loop(1, 8, lambda i: wo_copy(i, (y - i + 8) % 8, half_z).wait_recv())
 
@@ -382,16 +413,6 @@
         for n, s in enumerate(steps):
             wo2_copy(n, z_dev(s), my_quarter).start()
 
-    def make_kv(b, carry):
-        raw_kv[b] = jnp.dot(ut[256:384, :], hot[b], preferred_element_type=F32)
-        return carry
-
-    def make_q(zb, carry):
-        raw_q[zb] = jnp.dot(ut[:256, :], hot[zb * 4 + x], preferred_element_type=F32)
-        return carry
-
-    lax.fori_loop(0, NCTX, make_kv, 0)
-    lax.fori_loop(0, 4, make_q, 0)
     loop(1, 16, lambda i: sc_copy(i, (c - i + NCTX) % NCTX).wait_recv())
 
     def turn(v, b, scale_row):
@@ -458,7 +479,8 @@
             [(jnp.full((1, BLK), masked_score, F32), jnp.zeros((80, BLK), F32)) for _ in range(4)],
             [scores(zb, 0, h) for h in range(4)],
         )
-        carry = lax.fori_loop(0, zb, four, carry)
+        for j in range(zb):
+            carry = four(j, carry)
         for k in range(4):
             carry = one(4 * zb + k, carry, k)
         for h in range(4):
@@ -492,54 +514,43 @@
     lax.fori_loop(1, 5, block_step, 0)
     att_in[zl] = att_out[zl]
 
-    ref = wo.at[:, :, 1 - core]
-    rc(ref, ref, wo3_s.at[0], wo3_r.at[0], (sib, c)).wait_recv()
-    for i in (1, 2, 3):
-        slot = (zl - i + 4) % 4
-        att_copy(slot, slot).wait_recv()
-
-    attended = att_in[...].reshape(D, BLK)
-    pick = (align_ref[...] - c * BLK == lax.broadcasted_iota(jnp.int32, (BLK, BLK), 0)).astype(BF16)
-    total = jnp.zeros((BLK, 1), F32)
-    for j in range(4):
-        cols = pl.ds(j * 256, 256)
-        branch = tn(attended, wo[j].reshape(D, 256))
-        hidden = (lat_scr[:, cols].astype(F32) + branch).astype(BF16)
-        hid_ref[:, cols] = hidden
-        diff = tn(pick, hidden) - teach_ref[:, cols].astype(F32)
-        total = total + jnp.sum(diff * diff, axis=1, keepdims=True)
-    loss_ref[...] = jnp.broadcast_to(total * (1.0 / D), (BLK, 128)).T[0:1, :]
-
-    for d in range(1, 4):
-        wc_copy(d, my_slot).wait_send()
-
     @pl.when(at_edge)
     def _():
         for t in (1, 2):
-            for d in range(4):
-                wc_near(t, d, my_slot).wait_send()
             wq_near(t, y * 2 + zh).wait_send()
             wo_near(t, y * 2 + zh).wait_send()
 
-    loop(1, 16, lambda i: ids_copy(i, c).wait_send())
     loop(1, 16, lambda i: sc_copy(i, c).wait_send())
     for half_z in (0, 1):
         loop(1, 8, lambda i: wg_copy(i, y, half_z).wait_send())
         loop(1, 8, lambda i: wo_copy(i, y, half_z).wait_send())
 
-    @pl.when(tap // 2 == core)
-    def _():
-        for step in (1, 2, 3):
-            y_copy(step, tap).wait_send()
-
     for n, s in enumerate(steps):
-        first_copy(n, z_dev(s), own).wait_send()
         wo2_copy(n, x_dev(s), my_quarter).wait_send()
     for n in range(6):
         along_x(n, 0).wait_send()
     for n in range(4):
         over(n, slice_x(0, core)).wait_send()
     rc(wg.at[:, core], wg.at[:, core], wgx_s.at[0], wgx_r.at[0], (sib, c)).wait_send()
+
+    ref = wo.at[:, :, 1 - core]
+    rc(ref, ref, wo3_s.at[0], wo3_r.at[0], (sib, c)).wait_recv()
+    for i in (1, 2, 3):
+        slot = (zl - i + 4) % 4
+        att_copy(slot, slot).wait_recv()
+
+    attended = att_in[...].reshape(D, BLK).T
+    pick = (align_ref[...] - c * BLK == lax.broadcasted_iota(jnp.int32, (BLK, BLK), 0)).astype(BF16)
+    total = jnp.zeros((BLK, 1), F32)
+    for j in range(4):
+        cols = pl.ds(j * 256, 256)
+        branch = jnp.dot(attended, wo[j].reshape(D, 256), preferred_element_type=F32)
+        hidden = (lat_scr[:, cols].astype(F32) + branch).astype(BF16)
+        hid_ref[:, cols] = hidden
+        diff = tn(pick, hidden) - teach_ref[:, cols].astype(F32)
+        total = total + jnp.sum(diff * diff, axis=1, keepdims=True)
+    loss_ref[...] = jnp.broadcast_to(total * (1.0 / D), (BLK, 128)).T[0:1, :]
+
     rc(wo.at[:, :, core], wo.at[:, :, core], wo3_s.at[0], wo3_r.at[0], (sib, c)).wait_send()
     for i in (1, 2, 3):
         att_copy((zl + i) % 4, zl).wait_send()

time: 77.8 us -> 82.3 us (1.058)
  the two profiles are of different devices: /device:TPU:43 before, /device:TPU:249 now
where the time goes in v4:
time: 82.3 us; the launch traced here: 82.1 us
  Pallas kernels  79 us (96%)
  local copies, waits for them, and re-layouts  2.44 us (3%)
    pallas_call x1, Pallas kernels, body(): pl.pallas_call(kernel, out_shape=(jax.ShapeDtypeStruct((BLK, D), BF16), j...  79 us
    unnamed x4, local copies, waits for them, and re-layouts  2.44 us

profile of v4, /device:TPU:249, one launch (start us, length us, event | category | flops | bytes accessed | tf_op | source)
XLA Modules:
  0.0 82.1 jit_solution(10457933841574374297)
XLA Ops:
  0.6 79.0 %shard_map.113 = (bf16[256,1024]{1,0:T(8,128)(2,1)}, f32[1,256]{1,0:T(1,128)}) custom-call(s32[1,1024]{1,0:T(1,128)} %ids_ref.1, bf16[256,768]{1,0:T(8,128)(2,1)} %bt_ref.1, bf16[96,1024]{1,0:T(8,128)(2,1)} %wconv_ref.1, bf16[32,1536]{1,0:T(8,128)(2,1)} %wqkv_ref.1, bf16[32,1024]{1,0:T(8,128)(2,1)} %wo_ref.1, bf16[8,128]{1,0:T(8,128)(2,1)} %bitcast.5, ...), custom_call_target="tpu_custom_call" | custom-call | tf_op jit(solution)/shard_map/pallas_call | solution.py:563
  79.7 0.0 copy-start
  79.7 1.9 %copy.14 = bf16[1,256,1024]{2,1,0:T(8,128)(2,1)} copy(bf16[1,256,1024]{2,1,0:T(8,128)(2,1)} %bitcast.4) | data formatting | bytes 1048576
  81.5 0.0 copy-done
  81.5 0.6 copy.15
Async XLA Ops:
  79.7 1.9 %copy-start = (f32[1,256]{1,0:T(1,128)S(1)}, f32[1,256]{1,0:T(1,128)}, u32[]{:S(2)}) copy-start(f32[1,256]{1,0:T(1,128)} %get-tuple-element.9) | copy-start | bytes 3076

commit v5 on v4

--- a/solution.py
+++ b/solution.py
@@ -267,7 +267,6 @@
         return carry
 
     def meanwhile():
-        loop(1, 8, lambda i: wo_copy(i, y, zh).start())
         rc(
             wo_cols(zl), wo.at[my_quarter, y * 2 + 1 - zh, core], wo_s.at[16], wo_r.at[16], z_dev(1)
         ).wait_recv()
@@ -322,6 +321,7 @@
     def _():
         for n, s in enumerate(steps):
             first_copy(n, z_dev(s), own).start()
+        loop(1, 8, lambda i: wo_copy(i, y, zh).start())
         for n, s in enumerate(steps):
             first_copy(n, z_dev(s), tt.at[core, (zl - s + 4) % 4, x]).wait_recv()
         for n in (0, 1, 2, 3):
@@ -331,6 +331,7 @@
     def _():
         for n, s in enumerate(steps):
             first_copy(n, x_dev(s), own).start()
+        loop(1, 8, lambda i: wo_copy(i, y, zh).start())
         for n, s in enumerate(steps):
             first_copy(n, x_dev(s), tt.at[core, zl, (x - s + 4) % 4]).wait_recv()
         for n in (0, 1, 2, 3):
@@ -385,6 +386,24 @@
     for part in (0, 1):
         ut[:, part * 512 : (part + 1) * 512] = tn(wgt, table(part)).astype(BF16)
 
+    for half_z in (0, 1):
+        loop(1, 8, lambda i: wo_copy(i, (y - i + 8) % 8, half_z).wait_recv())
+    far_steps = ((1, 0, 16), (-1, 0, 16), (2, 0, 8), (-2, 8, 8))
+
+    def wo2_copy(n, dev, slot):
+        ref = wo.at[slot, pl.ds(far_steps[n][1], far_steps[n][2]), core]
+        return rc(ref, ref, wo2_s.at[n], wo2_r.at[n], dev)
+
+    @pl.when(core == 0)
+    def _():
+        for n, s in enumerate(far_steps):
+            wo2_copy(n, x_dev(s[0]), my_quarter).start()
+
+    @pl.when(core == 1)
+    def _():
+        for n, s in enumerate(far_steps):
+            wo2_copy(n, z_dev(s[0]), my_quarter).start()
+
     def make_kv(b, carry):
         raw_kv[b] = jnp.dot(ut[256:384, :], hot[b], preferred_element_type=F32)
         return carry
@@ -395,23 +414,6 @@
 
     lax.fori_loop(0, NCTX, make_kv, 0)
     lax.fori_loop(0, 4, make_q, 0)
-
-    for half_z in (0, 1):
-        loop(1, 8, lambda i: wo_copy(i, (y - i + 8) % 8, half_z).wait_recv())
-
-    def wo2_copy(n, dev, slot):
-        ref = wo.at[slot, :, core]
-        return rc(ref, ref, wo2_s.at[n], wo2_r.at[n], dev)
-
-    @pl.when(core == 0)
-    def _():
-        for n, s in enumerate(steps):
-            wo2_copy(n, x_dev(s), my_quarter).start()
-
-    @pl.when(core == 1)
-    def _():
-        for n, s in enumerate(steps):
-            wo2_copy(n, z_dev(s), my_quarter).start()
 
     loop(1, 16, lambda i: sc_copy(i, (c - i + NCTX) % NCTX).wait_recv())
 
@@ -495,8 +497,8 @@
 
         @pl.when(i == 3)
         def _():
-            for n, s in enumerate(steps):
-                wo2_copy(n, x_dev(s), (my_quarter - s + 4) % 4).wait_recv()
+            for n, s in enumerate(far_steps):
+                wo2_copy(n, x_dev(s[0]), (my_quarter - s[0] + 4) % 4).wait_recv()
             rc(wo.at[:, :, core], wo.at[:, :, core], wo3_s.at[0], wo3_r.at[0], (sib, c)).start()
 
         for k in range(4):
@@ -525,8 +527,8 @@
         loop(1, 8, lambda i: wg_copy(i, y, half_z).wait_send())
         loop(1, 8, lambda i: wo_copy(i, y, half_z).wait_send())
 
-    for n, s in enumerate(steps):
-        wo2_copy(n, x_dev(s), my_quarter).wait_send()
+    for n, s in enumerate(far_steps):
+        wo2_copy(n, x_dev(s[0]), my_quarter).wait_send()
     for n in range(6):
         along_x(n, 0).wait_send()
     for n in range(4):
@@ -596,7 +598,7 @@
         ]
         + [
             dma((n,))
-            for n in (16, 16, 16, 16, 12, 8, 4, 4, 3, 3, 6, 6, 4, 4, 18, 17, 1, 1, 18, 17, 3, 3, 1, 1, 4, 4)
+            for n in (16, 16, 16, 16, 12, 8, 4, 4, 3, 3, 6, 6, 4, 4, 18, 17, 1, 1, 18, 17, 4, 4, 1, 1, 4, 4)
         ],
         compiler_params=pltpu.CompilerParams(
             collective_id=0, has_side_effects=True, vmem_limit_bytes=56 * 2**20

time: 82.3 us -> 77.8 us (0.945)
  the two profiles are of different devices: /device:TPU:249 before, /device:TPU:43 now
where the time goes in v5:
time: 77.8 us; the launch traced here: 77.6 us
  Pallas kernels  74.5 us (96%)
  local copies, waits for them, and re-layouts  2.44 us (3%)
    pallas_call x1, Pallas kernels, body(): pl.pallas_call(kernel, out_shape=(jax.ShapeDtypeStruct((BLK, D), BF16), j...  74.5 us
    unnamed x4, local copies, waits for them, and re-layouts  2.44 us

profile of v5, /device:TPU:43, one launch (start us, length us, event | category | flops | bytes accessed | tf_op | source)
XLA Modules:
  0.0 77.6 jit_solution(17134120927053109144)
XLA Ops:
  0.6 74.5 %shard_map.113 = (bf16[256,1024]{1,0:T(8,128)(2,1)}, f32[1,256]{1,0:T(1,128)}) custom-call(s32[1,1024]{1,0:T(1,128)} %ids_ref.1, bf16[256,768]{1,0:T(8,128)(2,1)} %bt_ref.1, bf16[96,1024]{1,0:T(8,128)(2,1)} %wconv_ref.1, bf16[32,1536]{1,0:T(8,128)(2,1)} %wqkv_ref.1, bf16[32,1024]{1,0:T(8,128)(2,1)} %wo_ref.1, bf16[8,128]{1,0:T(8,128)(2,1)} %bitcast.5, ...), custom_call_target="tpu_custom_call" | custom-call | tf_op jit(solution)/shard_map/pallas_call | solution.py:565
  75.2 0.0 copy-start
  75.2 1.9 %copy.14 = bf16[1,256,1024]{2,1,0:T(8,128)(2,1)} copy(bf16[1,256,1024]{2,1,0:T(8,128)(2,1)} %bitcast.4) | data formatting | bytes 1048576
  77.1 0.0 copy-done
  77.1 0.6 copy.15
Async XLA Ops:
  75.2 1.9 %copy-start = (f32[1,256]{1,0:T(1,128)S(1)}, f32[1,256]{1,0:T(1,128)}, u32[]{:S(2)}) copy-start(f32[1,256]{1,0:T(1,128)} %get-tuple-element.9) | copy-start | bytes 3076

commit v6 on v5

--- a/solution.py
+++ b/solution.py
@@ -493,7 +493,7 @@
         return rc(att_out.at[zb], att_in.at[slot], at_s.at[zb], at_r.at[slot], (f, zb * 4 + x))
 
     def block_step(i, carry):
-        zb = (zl + i) % 4
+        zb = (zl - i + 8) % 4
 
         @pl.when(i == 3)
         def _():

time: 77.8 us -> 76.7 us (0.986)
  Pallas kernels: 74.5 us -> 73.5 us
    pallas_call x1, Pallas kernels: 74.5 us -> 73.5 us  [body(): pl.pallas_call(kernel, out_shape=(jax.ShapeDtypeStruct((BLK, D), BF16), j...]
where the time goes in v6:
time: 76.7 us; the launch traced here: 76.5 us
  Pallas kernels  73.5 us (96%)
  local copies, waits for them, and re-layouts  2.44 us (3%)
    pallas_call x1, Pallas kernels, body(): pl.pallas_call(kernel, out_shape=(jax.ShapeDtypeStruct((BLK, D), BF16), j...  73.5 us
    unnamed x4, local copies, waits for them, and re-layouts  2.44 us

profile of v6, /device:TPU:43, one launch (start us, length us, event | category | flops | bytes accessed | tf_op | source)
XLA Modules:
  0.0 76.5 jit_solution(9989944870279562926)
XLA Ops:
  0.6 73.5 %shard_map.113 = (bf16[256,1024]{1,0:T(8,128)(2,1)}, f32[1,256]{1,0:T(1,128)}) custom-call(s32[1,1024]{1,0:T(1,128)} %ids_ref.1, bf16[256,768]{1,0:T(8,128)(2,1)} %bt_ref.1, bf16[96,1024]{1,0:T(8,128)(2,1)} %wconv_ref.1, bf16[32,1536]{1,0:T(8,128)(2,1)} %wqkv_ref.1, bf16[32,1024]{1,0:T(8,128)(2,1)} %wo_ref.1, bf16[8,128]{1,0:T(8,128)(2,1)} %bitcast.5, ...), custom_call_target="tpu_custom_call" | custom-call | tf_op jit(solution)/shard_map/pallas_call | solution.py:565
  74.1 0.0 copy-start
  74.1 1.9 %copy.14 = bf16[1,256,1024]{2,1,0:T(8,128)(2,1)} copy(bf16[1,256,1024]{2,1,0:T(8,128)(2,1)} %bitcast.4) | data formatting | bytes 1048576
  76.0 0.0 copy-done
  76.0 0.6 copy.15
Async XLA Ops:
  74.1 1.9 %copy-start = (f32[1,256]{1,0:T(1,128)S(1)}, f32[1,256]{1,0:T(1,128)}, u32[]{:S(2)}) copy-start(f32[1,256]{1,0:T(1,128)} %get-tuple-element.9) | copy-start | bytes 3076

commit v7 on v6

--- a/solution.py
+++ b/solution.py
@@ -382,9 +382,9 @@
 
     ref = wg.at[:, 1 - core]
     rc(ref, ref, wgx_s.at[0], wgx_r.at[0], (sib, c)).wait_recv()
-    wgt = wg[...].reshape(D, 384)
+    wgt = wg[...].reshape(D, 384).T
     for part in (0, 1):
-        ut[:, part * 512 : (part + 1) * 512] = tn(wgt, table(part)).astype(BF16)
+        ut[:, part * 512 : (part + 1) * 512] = jnp.dot(wgt, table(part), preferred_element_type=F32).astype(BF16)
 
     for half_z in (0, 1):
         loop(1, 8, lambda i: wo_copy(i, (y - i + 8) % 8, half_z).wait_recv())
@@ -515,6 +515,7 @@
 
     lax.fori_loop(1, 5, block_step, 0)
     att_in[zl] = att_out[zl]
+    pick = (align_ref[...] - c * BLK == lax.broadcasted_iota(jnp.int32, (BLK, BLK), 0)).astype(BF16).T
 
     @pl.when(at_edge)
     def _():
@@ -542,14 +543,13 @@
         att_copy(slot, slot).wait_recv()
 
     attended = att_in[...].reshape(D, BLK).T
-    pick = (align_ref[...] - c * BLK == lax.broadcasted_iota(jnp.int32, (BLK, BLK), 0)).astype(BF16)
     total = jnp.zeros((BLK, 1), F32)
     for j in range(4):
         cols = pl.ds(j * 256, 256)
         branch = jnp.dot(attended, wo[j].reshape(D, 256), preferred_element_type=F32)
         hidden = (lat_scr[:, cols].astype(F32) + branch).astype(BF16)
         hid_ref[:, cols] = hidden
-        diff = tn(pick, hidden) - teach_ref[:, cols].astype(F32)
+        diff = jnp.dot(pick, hidden, preferred_element_type=F32) - teach_ref[:, cols].astype(F32)
         total = total + jnp.sum(diff * diff, axis=1, keepdims=True)
     loss_ref[...] = jnp.broadcast_to(total * (1.0 / D), (BLK, 128)).T[0:1, :]
 

time: 76.7 us -> 76.7 us (level)
  no operation moved by 1% of the time
where the time goes in v7:
time: 76.7 us; the launch traced here: 76.5 us
  Pallas kernels  73.5 us (96%)
  local copies, waits for them, and re-layouts  2.44 us (3%)
    pallas_call x1, Pallas kernels, body(): pl.pallas_call(kernel, out_shape=(jax.ShapeDtypeStruct((BLK, D), BF16), j...  73.5 us
    unnamed x4, local copies, waits for them, and re-layouts  2.44 us

profile of v7, /device:TPU:43, one launch (start us, length us, event | category | flops | bytes accessed | tf_op | source)
XLA Modules:
  0.0 76.5 jit_solution(4643751190604368513)
XLA Ops:
  0.6 73.5 %shard_map.113 = (bf16[256,1024]{1,0:T(8,128)(2,1)}, f32[1,256]{1,0:T(1,128)}) custom-call(s32[1,1024]{1,0:T(1,128)} %ids_ref.1, bf16[256,768]{1,0:T(8,128)(2,1)} %bt_ref.1, bf16[96,1024]{1,0:T(8,128)(2,1)} %wconv_ref.1, bf16[32,1536]{1,0:T(8,128)(2,1)} %wqkv_ref.1, bf16[32,1024]{1,0:T(8,128)(2,1)} %wo_ref.1, bf16[8,128]{1,0:T(8,128)(2,1)} %bitcast.5, ...), custom_call_target="tpu_custom_call" | custom-call | tf_op jit(solution)/shard_map/pallas_call | solution.py:565
  74.1 0.0 copy-start
  74.1 1.9 %copy.14 = bf16[1,256,1024]{2,1,0:T(8,128)(2,1)} copy(bf16[1,256,1024]{2,1,0:T(8,128)(2,1)} %bitcast.4) | data formatting | bytes 1048576
  76.0 0.0 copy-done
  76.0 0.6 copy.15
Async XLA Ops:
  74.1 1.9 %copy-start = (f32[1,256]{1,0:T(1,128)S(1)}, f32[1,256]{1,0:T(1,128)}, u32[]{:S(2)}) copy-start(f32[1,256]{1,0:T(1,128)} %get-tuple-element.9) | copy-start | bytes 3076
